TPU v7x, 256 devices: a whole 4x4x8 slice. The times are simulated.
256 devices in a mesh: row: 8 (over z), col: 32 (over y, x, core).
Axes of the slice: x: 4, y: 4, z: 8, core: 2. Of those that a mesh axis runs over, the one named last changes fastest.
Arguments:
- positions: float32 [3, 6291456], P(None, ('row', 'col')), may hold values from -10 to 10
- moments: float32 [3, 6291456], P(None, ('row', 'col')), may hold values from -6 to 6
- near_list: int32 [49152, 2], P(('row', 'col')), may hold values from 0 to 575
- far_list: int32 [49152, 16], P(('row', 'col')), may hold values from 0 to 1023
- let_rows: int32 [256, 8, 128], P(('row', 'col')), may hold values from 0 to 191
Outputs:
- near_field: float32 [3, 6291456], P(None, ('row', 'col'))
- let_field: float32 [3, 6291456], P(None, ('row', 'col'))
- top_field: float32 [3, 6291456], P(None, ('row', 'col'))
All inputs are finite; a program needn't handle non-finite values.
Results may differ from a plain program's by a relative error of at most 0.0003.
Values sent between devices are 32-bit elements; how exact they have to be, the bound alone decides.
A program may use at most 64 MiB of HBM per device.

v0:
```python
import functools

import jax
import jax.numpy as jnp
from jax import lax
from jax.experimental import pallas as pl
from jax.experimental.pallas import tpu as pltpu
from jax.sharding import PartitionSpec as P

CELL = 128
SOFTEN = 0.09
COUPLING = 0.004
F32 = jnp.float32
BF16 = jnp.bfloat16
MESH = pl.DeviceIdType.MESH
HIGHEST = lax.Precision.HIGHEST
VMEM_LIMIT = 58 * 1024 * 1024
SIX = ((0, 0), (0, 1), (0, 2), (1, 1), (1, 2), (2, 2))
NEAR_K = 48
FAR_K = 64
OUT_K = 16
NEAR_S = 56
FAR_S = 72
COEF_S = 56
TOP_UNROLL = 24
NEAR_UNROLL = 16


def split3(value):
    high = value.astype(BF16).astype(F32)
    rest = value - high
    middle = rest.astype(BF16).astype(F32)
    return high, middle, rest - middle


def split2(value):
    high = value.astype(BF16)
    return high, (value - high.astype(F32)).astype(BF16)


def source_pairing(parts):
    return [parts[0], parts[1], parts[2], parts[0], parts[1], parts[0]]


def target_pairing(parts):
    return [parts[0], parts[0], parts[0], parts[1], parts[1], parts[2]]


def expansion_coefficients(table):
    c = table[0:3]
    m = [COUPLING * entry for entry in table[3:6]]
    q = [[COUPLING * table[6 + 3 * j + i] for i in range(3)] for j in range(3)]
    g = [[q[j][i] + q[i][j] for i in range(3)] for j in range(3)]
    t = q[0][0] + q[1][1] + q[2][2]
    gc = [g[i][0] * c[0] + g[i][1] * c[1] + g[i][2] * c[2] for i in range(3)]
    zero = jnp.zeros_like(c[0])
    one = jnp.ones_like(c[0])
    square = (
        c[0] * c[0] + c[1] * c[1] + c[2] * c[2] + SOFTEN,
        [-2.0 * c[i] for i in range(3)],
        [one if i == j else zero for i, j in SIX],
    )
    first = (
        -3.0 * (c[0] * m[0] + c[1] * m[1] + c[2] * m[2] + t),
        [3.0 * m[i] for i in range(3)],
        None,
    )
    second = (
        7.5 * (c[0] * gc[0] + c[1] * gc[1] + c[2] * gc[2]),
        [-15.0 * gc[i] for i in range(3)],
        [(7.5 if i == j else 15.0) * g[i][j] for i, j in SIX],
    )
    outputs = [one] + list(c) + m + [3.0 * g[i][j] for i, j in SIX] + [3.0 * gc[i] for i in range(3)]
    return square, first, second, outputs


def source_rows(form, zero):
    const, linear, quadratic = form
    rows = list(split3(const))
    for entry in linear:
        rows += source_pairing(split3(entry))
    if quadratic is None:
        rows += [zero] * 36
    else:
        for entry in quadratic:
            rows += source_pairing(split3(entry))
    return rows + [zero] * (FAR_K - len(rows))


def target_rows(x):
    one = jnp.ones_like(x[0])
    rows = [one, one, one]
    for entry in x:
        rows += target_pairing(split3(entry))
    for i, j in SIX:
        rows += target_pairing(split3(x[i] * x[j]))
    return rows + [jnp.zeros_like(one)] * (FAR_K - len(rows))


def weights_of(square, first, second):
    inverse = lax.rsqrt(square)
    two = inverse * inverse
    three = two * inverse
    five = three * two
    return five * (first + second * two), three, five


def expansion_fields(x, sums):
    g = {}
    for place, (i, j) in enumerate(SIX):
        g[i, j] = g[j, i] = sums[7 + place]
    return [
        x[i] * sums[0]
        - sums[1 + i]
        - sums[4 + i]
        - (g[i, 0] * x[0] + g[i, 1] * x[1] + g[i, 2] * x[2])
        + sums[13 + i]
        for i in range(3)
    ]


def pitch_of(cells):
    return cells + 8 * (1 - cells // 8 % 2)


def rows8(start):
    return pl.ds(pl.multiple_of(start, 8), 8)


def lanes(block):
    return pl.ds(pl.multiple_of(block * CELL, CELL), CELL)


def store_rows(ref, rows, first, stride):
    for place, value in enumerate(rows):
        ref[pl.ds(first * stride + place, 8, stride=stride), :] = value


def own_offsets(planes_ref, centre_ref, cells, start):
    return [
        planes_ref[rows8(i * pitch_of(cells) + start), :] - centre_ref[i : i + 1, :] for i in range(3)
    ]


def planes_to_output(planes_ref, out_ref, cells):
    def step(b, carry):
        out_ref[:, lanes(b)] = planes_ref[pl.ds(b, 3, stride=pitch_of(cells)), :]
        return carry

    lax.fori_loop(0, cells, step, 0, unroll=8)


def leaf_sections(cells, place, moment, let_rows_ref, let_ref):
    ones = jnp.ones((CELL, CELL), F32)
    eight = jnp.ones((8, CELL), F32)
    padding = jnp.zeros((256 - cells, CELL), F32)

    def lane_sums(plane):
        return lax.dot_general(
            eight,
            jnp.concatenate([plane, padding], axis=0),
            (((1,), (1,)), ((), ())),
            precision=HIGHEST,
            preferred_element_type=F32,
        )

    spread = [
        entry - jnp.dot(entry, ones, precision=HIGHEST, preferred_element_type=F32) * (1.0 / CELL)
        for entry in place
    ]
    leaf = [lane_sums(entry) * (1.0 / CELL) for entry in place]
    leaf += [lane_sums(entry) for entry in moment]
    leaf += [lane_sums(spread[j] * moment[i]) for j in range(3) for i in range(3)]
    chosen = let_rows_ref[0]
    low = jnp.bitwise_and(chosen, CELL - 1)
    upper = chosen >= CELL
    for entry in range(15):
        let_ref[:, entry, :] = jnp.where(
            upper,
            jnp.take_along_axis(leaf[entry][:, CELL:], low, axis=1),
            jnp.take_along_axis(leaf[entry][:, :CELL], low, axis=1),
        )
    let_ref[:, 15, :] = jnp.zeros((8, CELL), F32)


def top_tables(cells, place, moment, top_ref, centre_ref):
    half = cells // 2
    sublane = lax.broadcasted_iota(jnp.int32, (8, CELL), 0)
    lane = lax.broadcasted_iota(jnp.int32, (8, CELL), 1)
    tile = jnp.zeros((8, CELL), F32)
    centres = []

    def total(plane):
        column = jnp.sum(plane, axis=0, keepdims=True)
        return jnp.sum(column, axis=1, keepdims=True)

    for top in range(2):
        part = slice(top * half, (top + 1) * half)
        centre = [total(place[i][part]) * (1.0 / (half * CELL)) for i in range(3)]
        entries = list(centre) + [total(moment[i][part]) for i in range(3)]
        for j in range(3):
            offset = place[j][part] - centre[j]
            entries += [total(offset * moment[i][part]) for i in range(3)]
        for entry in range(15):
            tile = jnp.where((sublane == top) & (lane == entry), entries[entry], tile)
        centres.append(centre)
    top_ref[...] = tile
    middle = jnp.zeros((8, CELL), F32)
    for i in range(3):
        middle = jnp.where(sublane == i, 0.5 * (centres[0][i] + centres[1][i]), middle)
    centre_ref[...] = middle


def first_kernel(
    cells,
    n_row,
    n_col,
    pos_ref,
    mom_ref,
    let_rows_ref,
    planes_ref,
    before_ref,
    after_ref,
    let_in,
    centre_ref,
    out_ref,
    let_ref,
    top_ref,
    top_in,
    feats,
    forms_rows,
    forms,
    coeffs,
    sums,
    field,
    side_send,
    side_recv,
    let_send,
    let_recv,
    top_send,
    top_recv,
):
    row = lax.axis_index("row")
    col = lax.axis_index("col")
    device = row * n_col + col
    devices = n_row * n_col
    col_bits = n_col.bit_length() - 1
    row_bits = n_row.bit_length() - 1
    sources = 2 * n_col
    pitch = pitch_of(cells)

    def flip(value, bit):
        return value + (1 << bit) * (1 - 2 * lax.rem(value // (1 << bit), 2))

    def place_of(index):
        return (index // n_col, lax.rem(index, n_col))

    following = place_of(lax.rem(device + 1, devices))
    preceding = place_of(lax.rem(device + devices - 1, devices))

    barrier = pltpu.get_barrier_semaphore()

    def greet(step, carry):
        other = lax.rem(col + step, n_col)
        pl.semaphore_signal(barrier, inc=1, device_id=(row, other), device_id_type=MESH)
        return carry

    lax.fori_loop(1, n_col, greet, 0)
    for bit in range(row_bits):
        pl.semaphore_signal(barrier, inc=1, device_id=(flip(row, bit), col), device_id_type=MESH)

    @pl.when(col == 0)
    def _():
        pl.semaphore_signal(barrier, inc=1, device_id=preceding, device_id_type=MESH)

    @pl.when(col == n_col - 1)
    def _():
        pl.semaphore_signal(barrier, inc=1, device_id=following, device_id_type=MESH)

    def to_planes(b, carry):
        planes_ref[pl.ds(b, 3, stride=pitch), :] = pos_ref[:, lanes(b)]
        planes_ref[pl.ds(3 * pitch + b, 3, stride=pitch), :] = mom_ref[:, lanes(b)]
        return carry

    lax.fori_loop(0, cells, to_planes, 0, unroll=8)
    top_in[col] = jnp.zeros(top_ref.shape, F32)

    edge = jnp.where(col == 0, 1, 0) + jnp.where(col == n_col - 1, 1, 0)
    pl.semaphore_wait(barrier, n_col - 1 + row_bits + edge)

    def side_copy(side, target, to):
        return pltpu.make_async_remote_copy(
            src_ref=planes_ref,
            dst_ref=target,
            send_sem=side_send.at[side],
            recv_sem=side_recv.at[side],
            device_id=to,
            device_id_type=MESH,
        )

    sides = [side_copy(0, before_ref, following), side_copy(1, after_ref, preceding)]
    for copy in sides:
        copy.start()

    place = [planes_ref[i * pitch : i * pitch + cells, :] for i in range(3)]
    moment = [planes_ref[(3 + i) * pitch : (3 + i) * pitch + cells, :] for i in range(3)]
    top_tables(cells, place, moment, top_ref, centre_ref)

    def top_copy(step):
        return pltpu.make_async_remote_copy(
            src_ref=top_ref,
            dst_ref=top_in.at[col],
            send_sem=top_send.at[step],
            recv_sem=top_recv.at[step],
            device_id=(row, lax.rem(col + step, n_col)),
            device_id_type=MESH,
        )

    def start(step, carry):
        top_copy(step).start()
        return carry

    def finish(step, carry):
        top_copy(step).wait()
        return carry

    lax.fori_loop(1, n_col, start, 0)

    leaf_sections(cells, place, moment, let_rows_ref, let_ref)
    sections = []
    for section in range(col_bits + row_bits):
        if section < col_bits:
            partner = (row, flip(col, section))
        else:
            partner = (flip(row, section - col_bits), col)
        sections.append(
            pltpu.make_async_remote_copy(
                src_ref=let_ref.at[section],
                dst_ref=let_in.at[section],
                send_sem=let_send.at[section],
                recv_sem=let_recv.at[section],
                device_id=partner,
                device_id_type=MESH,
            )
        )
    for copy in sections:
        copy.start()

    def build(group, carry):
        x = own_offsets(planes_ref, centre_ref, cells, group * 8)
        store_rows(feats, target_rows(x), group * 8, FAR_S)
        return carry

    lax.fori_loop(0, cells // 8, build, 0)
    lax.fori_loop(1, n_col, finish, 0)

    table = jnp.concatenate(
        [top_in[:, top, :] for top in range(2)] + [jnp.zeros((CELL - sources, CELL), F32)], axis=0
    )
    table = table.T
    entries = [table[k : k + 1, :] for k in range(15)]
    entries = [entries[i] - centre_ref[i : i + 1, :] for i in range(3)] + entries[3:]
    square, first, second, outputs = expansion_coefficients(entries)
    zero = jnp.zeros_like(entries[0])
    for position, form in enumerate((square, first, second)):
        for k, value in enumerate(source_rows(form, zero)):
            forms_rows[position * FAR_K + k : position * FAR_K + k + 1, :] = value
    for position in range(3):
        forms[position * sources : (position + 1) * sources, :] = (
            forms_rows[position * FAR_K : (position + 1) * FAR_K, :].T[:sources, :].astype(BF16)
        )
    for k, value in enumerate(outputs):
        for part, piece in enumerate(split3(value)):
            forms_rows[part * OUT_K + k : part * OUT_K + k + 1, :] = piece
    stacked = forms_rows[0 : 3 * OUT_K, 0:sources]
    kind = lax.rem(lax.broadcasted_iota(jnp.int32, stacked.shape, 0), OUT_K)
    pieces = []
    for low, high in ((0, 4), (4, 7), (7, OUT_K)):
        piece = jnp.where((kind >= low) & (kind < high), stacked, 0.0)
        pieces += [piece, piece]
    coeffs[...] = jnp.concatenate(pieces, axis=1).astype(BF16)

    def step(pair, carry):
        for sub in range(TOP_UNROLL):
            cell = 2 * (TOP_UNROLL * pair + sub)
            features = jnp.concatenate(
                [
                    feats[pl.ds(pl.multiple_of((cell + k) * FAR_S, FAR_S), FAR_K), :]
                    for k in range(2)
                ],
                axis=1,
            ).astype(BF16)
            values = jnp.dot(forms[...], features, preferred_element_type=F32)
            parts = weights_of(
                values[:sources], values[sources : 2 * sources], values[2 * sources :]
            )
            weights = jnp.concatenate([half for part in parts for half in split2(part)], axis=0)
            result = jnp.dot(coeffs[...], weights, preferred_element_type=F32)
            result = result[:OUT_K] + result[OUT_K : 2 * OUT_K] + result[2 * OUT_K :]
            for k in range(2):
                sums[pl.ds(cell + k, OUT_K, stride=pitch), :] = result[:, k * CELL : (k + 1) * CELL]
        return carry

    lax.fori_loop(0, cells // (2 * TOP_UNROLL), step, 0)

    def finish_top(group, carry):
        x = own_offsets(planes_ref, centre_ref, cells, group * 8)
        totals = [sums[rows8(k * pitch + group * 8), :] for k in range(OUT_K)]
        for i, value in enumerate(expansion_fields(x, totals)):
            field[rows8(i * pitch + group * 8), :] = value
        return carry

    lax.fori_loop(0, cells // 8, finish_top, 0)
    planes_to_output(field, out_ref, cells)

    for copy in sections:
        copy.wait()
    for copy in sides:
        copy.wait()


def near_source_rows(y, moment):
    zero = jnp.zeros_like(y[0])
    one = jnp.ones_like(y[0])
    back = [split3(-2.0 * entry) for entry in y]
    square = split3(y[0] * y[0] + y[1] * y[1] + y[2] * y[2] + SOFTEN)
    scaled = [(3.0 * COUPLING) * entry for entry in moment]
    const = split3(-(y[0] * scaled[0] + y[1] * scaled[1] + y[2] * scaled[2]))
    scaled = [split3(entry) for entry in scaled]
    rows = []
    for part in range(3):
        rows += [one] + [b[part] for b in back] + [s[part] for s in scaled] + [const[part]]
    for part, source in ((0, 0), (1, 1), (2, 0)):
        rows += [square[part]] + [b[source] for b in back] + [s[source] for s in scaled] + [zero]
    return rows


def near_target_rows(x):
    one = jnp.ones_like(x[0])
    zero = jnp.zeros_like(x[0])
    norm = split3(x[0] * x[0] + x[1] * x[1] + x[2] * x[2])
    pieces = [split3(entry) for entry in x]
    rows = []
    for part in range(3):
        high = [p[0] for p in pieces]
        rows += [norm[part]] + high + high + [one]
    for target in (1, 1, 2):
        chosen = [p[target] for p in pieces]
        rows += [one] + chosen + chosen + [zero]
    return rows


def near_kernel(
    cells,
    devices,
    n_col,
    near_ref,
    own_ref,
    prev_ref,
    next_ref,
    centre_ref,
    far_ref,
    let_ref,
    near_out,
    let_out,
    near_sources,
    near_targets,
    far_sources,
    far_coeffs,
    far_targets,
    masks,
    near_sums,
    far_sums,
    field,
):
    sublane = lax.broadcasted_iota(jnp.int32, (8, CELL), 0)
    lane = lax.broadcasted_iota(jnp.int32, (8, CELL), 1)
    diagonal = lax.broadcasted_iota(jnp.int32, (CELL, CELL), 0) == lax.broadcasted_iota(
        jnp.int32, (CELL, CELL), 1
    )
    masks[0:CELL, :] = jnp.zeros((CELL, CELL), F32)
    masks[CELL : 2 * CELL, :] = jnp.where(diagonal, 1e30, 0.0)

    def build_sources(ref, first, keep):
        def build(group, carry):
            y = own_offsets(ref, centre_ref, cells, group * 8)
            moment = [ref[rows8((3 + i) * pitch_of(cells) + group * 8), :] for i in range(3)]
            if keep is not None:
                moment = [jnp.where(keep, entry, 0.0) for entry in moment]
            store_rows(near_sources, near_source_rows(y, moment), first + group * 8, NEAR_S)
            return carry

        lax.fori_loop(0, cells // 8, build, 0)

    device = lax.axis_index("row") * n_col + lax.axis_index("col")
    ordinal = jnp.full((8, CELL), device, jnp.int32)
    build_sources(prev_ref, 0, ordinal > 0)
    build_sources(own_ref, cells, None)
    build_sources(next_ref, 2 * cells, ordinal < devices - 1)

    def build_targets(group, carry):
        x = own_offsets(own_ref, centre_ref, cells, group * 8)
        store_rows(near_targets, near_target_rows(x), group * 8, NEAR_S)
        store_rows(far_targets, target_rows(x), group * 8, FAR_S)
        return carry

    lax.fori_loop(0, cells // 8, build_targets, 0)

    groups = cells // 8
    lists = far_ref[...].astype(F32)
    lists = jnp.concatenate([lists, jnp.zeros((lists.shape[0], 256 - cells), F32)], axis=1)
    lists = jnp.concatenate([lists, jnp.zeros((CELL - lists.shape[0], 256), F32)], axis=0)
    far_sums[0:256, :] = lists.T
    repeated = jnp.bitwise_and(lax.broadcasted_iota(jnp.int32, (groups, CELL), 1), 15)
    slot = jnp.right_shift(lax.broadcasted_iota(jnp.int32, (groups, CELL), 1), 4)
    listed = jnp.zeros((groups, CELL), F32)
    for k in range(8):
        rows = far_sums[pl.ds(k, groups, stride=8), :]
        listed = jnp.where(slot == k, jnp.take_along_axis(rows, repeated, axis=1), listed)
    listed = listed.astype(jnp.int32)
    low = jnp.bitwise_and(listed, CELL - 1)
    section = jnp.right_shift(listed, 7)
    dense = []
    for entry in range(15):
        table = let_ref[pl.ds(entry, 8, stride=16), :]
        value = jnp.zeros(listed.shape, F32)
        for k in range(8):
            source = jnp.broadcast_to(table[k : k + 1, :], listed.shape)
            value = jnp.where(section == k, jnp.take_along_axis(source, low, axis=1), value)
        dense.append(value)
    repeat = sublane * 16 + jnp.bitwise_and(lane, 15)
    for entry in range(15):
        far_sums[entry * groups : (entry + 1) * groups, :] = dense[entry]

    def build_far(group, carry):
        table = [
            jnp.take_along_axis(
                jnp.broadcast_to(far_sums[pl.ds(entry * groups + group, 1), :], (8, CELL)),
                repeat,
                axis=1,
            )
            for entry in range(15)
        ]
        table = [table[i] - centre_ref[i : i + 1, :] for i in range(3)] + table[3:]
        square, first, second, outputs = expansion_coefficients(table)
        zero = jnp.zeros((8, CELL), F32)
        forms = [source_rows(form, zero) for form in (square, first, second)]
        rows = [
            jnp.where(lane < 16, a, jnp.where(lane < 32, b, c)) for a, b, c in zip(*forms)
        ]
        store_rows(far_sources, rows, group * 8, FAR_S)
        pieces = [split3(value) for value in outputs]
        rows = []
        for part in range(3):
            for k in range(OUT_K):
                kind = 0 if k < 4 else 1 if k < 7 else 2
                inside = (lane >= 32 * kind) & (lane < 32 * kind + 32)
                rows.append(jnp.where(inside, pieces[k][part], 0.0))
        store_rows(far_coeffs, rows, group * 8, COEF_S)
        return carry

    lax.fori_loop(0, groups, build_far, 0)

    upper_rows = lax.rem(lax.broadcasted_iota(jnp.int32, (NEAR_K, CELL), 0), 8) < 4

    def near_part(cell):
        targets = near_targets[pl.ds(pl.multiple_of(cell * NEAR_S, NEAR_S), NEAR_K), :]
        features = jnp.concatenate(
            [jnp.where(upper_rows, targets, 0.0), jnp.where(upper_rows, 0.0, targets)], axis=1
        ).astype(BF16)
        total = None
        for e in range(2):
            block = near_ref[e, cell]
            source = near_sources[pl.ds(pl.multiple_of(block * NEAR_S, NEAR_S), NEAR_K), :]
            values = jnp.dot(source.astype(BF16).T, features, preferred_element_type=F32)
            own = (block == cells + cell).astype(jnp.int32)
            mask = masks[pl.ds(pl.multiple_of(own * CELL, CELL), CELL), :]
            inverse = lax.rsqrt(values[:, :CELL] + mask)
            two = inverse * inverse
            three = two * inverse
            projected = values[:, CELL:] * two * three
            p_high, p_low = split2(projected)
            t_high, t_low = split2(three)
            weights = jnp.concatenate(
                [
                    jnp.concatenate([p_high, t_high], axis=1),
                    jnp.concatenate([p_low, t_low], axis=1),
                ],
                axis=0,
            )
            coeffs = source[:32].astype(BF16)
            result = jnp.dot(
                jnp.concatenate([coeffs, coeffs], axis=1), weights, preferred_element_type=F32
            )
            result = result[0:8] + result[8:16] + result[16:24]
            total = result if total is None else total + result
        near_sums[pl.ds(cell, 8, stride=pitch_of(cells)), :] = jnp.where(
            sublane < 4, total[:, :CELL], total[:, CELL:]
        )

    def far_part(cell):
        source = far_sources[pl.ds(pl.multiple_of(cell * FAR_S, FAR_S), FAR_K), :]
        features = far_targets[pl.ds(pl.multiple_of(cell * FAR_S, FAR_S), FAR_K), :].astype(BF16)
        values = jnp.dot(source.astype(BF16).T[:48], features, preferred_element_type=F32)
        parts = weights_of(values[:16], values[16:32], values[32:48])
        weights = jnp.concatenate([half for part in parts for half in split2(part)], axis=0)
        coeffs = far_coeffs[pl.ds(pl.multiple_of(cell * COEF_S, COEF_S), 48), :][:, :96].astype(BF16)
        result = jnp.dot(coeffs, weights, preferred_element_type=F32)
        result = result[:OUT_K] + result[OUT_K : 2 * OUT_K] + result[2 * OUT_K :]
        far_sums[pl.ds(cell, OUT_K, stride=pitch_of(cells)), :] = result

    def step(pair, carry):
        for sub in range(NEAR_UNROLL):
            near_part(NEAR_UNROLL * pair + sub)
            far_part(NEAR_UNROLL * pair + sub)
        return carry

    lax.fori_loop(0, cells // NEAR_UNROLL, step, 0)

    def finish_near(group, carry):
        x = own_offsets(own_ref, centre_ref, cells, group * 8)
        totals = [near_sums[rows8(k * pitch_of(cells) + group * 8), :] for k in range(7)]
        for i in range(3):
            field[rows8(i * pitch_of(cells) + group * 8), :] = (
                (x[i] * totals[0] - totals[4 + i]) * (1.0 / 3.0) + 0.5 * totals[1 + i]
            )
        return carry

    lax.fori_loop(0, cells // 8, finish_near, 0)
    planes_to_output(field, near_out, cells)

    def finish_far(group, carry):
        x = own_offsets(own_ref, centre_ref, cells, group * 8)
        totals = [far_sums[rows8(k * pitch_of(cells) + group * 8), :] for k in range(OUT_K)]
        for i, value in enumerate(expansion_fields(x, totals)):
            field[rows8(i * pitch_of(cells) + group * 8), :] = value
        return carry

    lax.fori_loop(0, cells // 8, finish_far, 0)
    planes_to_output(field, let_out, cells)


def vmem(count):
    return [pl.BlockSpec(memory_space=pltpu.VMEM)] * count


def make_first(cells, n_row, n_col, n):
    bits = n_row.bit_length() + n_col.bit_length() - 2
    sources = 2 * n_col
    planes = jax.ShapeDtypeStruct((6 * pitch_of(cells), CELL), F32)
    return pl.pallas_call(
        functools.partial(first_kernel, cells, n_row, n_col),
        out_shape=(
            planes,
            planes,
            planes,
            jax.ShapeDtypeStruct((bits, 16, CELL), F32),
            jax.ShapeDtypeStruct((8, CELL), F32),
            jax.ShapeDtypeStruct((3, n), F32),
        ),
        in_specs=vmem(3),
        out_specs=tuple(
            vmem(1) + [pl.BlockSpec(memory_space=pl.ANY)] * 2 + vmem(3)
        ),
        scratch_shapes=[
            pltpu.VMEM((bits, 16, CELL), F32),
            pltpu.VMEM((8, CELL), F32),
            pltpu.VMEM((n_col, 8, CELL), F32),
            pltpu.VMEM((cells * FAR_S, CELL), F32),
            pltpu.VMEM((3 * FAR_K, CELL), F32),
            pltpu.VMEM((3 * sources, FAR_K), BF16),
            pltpu.VMEM((3 * OUT_K, 6 * sources), BF16),
            pltpu.VMEM((OUT_K * pitch_of(cells), CELL), F32),
            pltpu.VMEM((3 * pitch_of(cells), CELL), F32),
            pltpu.SemaphoreType.DMA((2,)),
            pltpu.SemaphoreType.DMA((2,)),
            pltpu.SemaphoreType.DMA((bits,)),
            pltpu.SemaphoreType.DMA((bits,)),
            pltpu.SemaphoreType.DMA((n_col,)),
            pltpu.SemaphoreType.DMA((n_col,)),
        ],
        compiler_params=pltpu.CompilerParams(
            collective_id=0, has_side_effects=True, vmem_limit_bytes=VMEM_LIMIT
        ),
        cost_estimate=pl.CostEstimate(
            flops=8_000_000_000, bytes_accessed=4_000_000, transcendentals=1_600_000
        ),
        name="tables_exchange_top",
    )


def make_near(cells, devices, n_col, n):
    return pl.pallas_call(
        functools.partial(near_kernel, cells, devices, n_col),
        out_shape=(jax.ShapeDtypeStruct((3, n), F32), jax.ShapeDtypeStruct((3, n), F32)),
        in_specs=[pl.BlockSpec(memory_space=pltpu.SMEM)] + vmem(6),
        out_specs=tuple(vmem(2)),
        scratch_shapes=[
            pltpu.VMEM((3 * cells * NEAR_S, CELL), F32),
            pltpu.VMEM((cells * NEAR_S, CELL), F32),
            pltpu.VMEM((cells * FAR_S, CELL), F32),
            pltpu.VMEM((cells * COEF_S, CELL), F32),
            pltpu.VMEM((cells * FAR_S, CELL), F32),
            pltpu.VMEM((2 * CELL, CELL), F32),
            pltpu.VMEM((8 * pitch_of(cells), CELL), F32),
            pltpu.VMEM((OUT_K * pitch_of(cells), CELL), F32),
            pltpu.VMEM((3 * pitch_of(cells), CELL), F32),
        ],
        compiler_params=pltpu.CompilerParams(vmem_limit_bytes=VMEM_LIMIT),
        cost_estimate=pl.CostEstimate(
            flops=30_000_000_000, bytes_accessed=4_000_000, transcendentals=6_600_000
        ),
        name="near_and_let_field",
    )


def body(positions, moments, near_list, far_list, let_rows):
    n = positions.shape[1]
    cells = n // CELL
    n_row, n_col = lax.axis_size("row"), lax.axis_size("col")
    bits = let_rows.shape[1]
    planes, before, after, let_in, centre, top = make_first(cells, n_row, n_col, n)(
        positions, moments, let_rows
    )
    near, remote = make_near(cells, n_row * n_col, n_col, n)(
        near_list.T,
        planes,
        before,
        after,
        centre,
        far_list.T,
        let_in.reshape(bits * 16, CELL),
    )
    return near, remote, top


def solution(mesh):
    return jax.shard_map(
        body,
        mesh=mesh,
        in_specs=(
            P(None, ("row", "col")),
            P(None, ("row", "col")),
            P(("row", "col"), None),
            P(("row", "col"), None),
            P(("row", "col"), None, None),
        ),
        out_specs=(P(None, ("row", "col")), P(None, ("row", "col")), P(None, ("row", "col"))),
        check_vma=False,
    )
```

profile of v0, /device:TPU:1, one launch (start us, length us, event | category | flops | bytes accessed | tf_op | source)
XLA Modules:
  0.0 66.3 jit_solution(13519724613707476512)
XLA Ops:
  0.6 33.0 %tables_exchange_top.1 = (f32[1200,128]{1,0:T(8,128)}, f32[1200,128]{1,0:T(8,128)}, f32[1200,128]{1,0:T(8,128)}, f32[8,16,128]{2,1,0:T(8,128)}, f32[8,128]{1,0:T(8,128)}, /*index=5*/f32[3,24576]{1,0:T(4,128)}) custom-call(f32[3,24576]{1,0:T(4,128)} %pos_ref.1, f32[3,24576]{1,0:T(4,128)} %mom_ref.1, s32[1,8,128]{2,1,0:T(8,128)} %let_rows_ref.1), custom_call_target="tpu_custom_call" | custom-call | flops 8000000000 | bytes 4000000 | tf_op jit(solution)/shard_map/tables_exchange_top/pallas_call | solution.py:722
  33.6 0.0 copy-start
  33.6 31.9 %near_and_let_field.1 = (f32[3,24576]{1,0:T(4,128)}, f32[3,24576]{1,0:T(4,128)}) custom-call(s32[2,192]{1,0:T(2,128)} %bitcast.4, f32[1200,128]{1,0:T(8,128)} %get-tuple-element.11.own_ref, f32[1200,128]{1,0:T(8,128)} %get-tuple-element.12.prev_ref, f32[1200,128]{1,0:T(8,128)} %get-tuple-element.13.next_ref, f32[8,128]{1,0:T(8,128)} %get-tuple-element.14.centre_ref, ...), custom_call_target="tpu_custom_call" | custom-call | flops 30000001024 | bytes 4000000 | tf_op jit(solution)/shard_map/near_and_let_field/pallas_call | solution.py:725
  65.5 0.0 copy-done
  65.5 0.7 %copy.9 = f32[3,24576]{1,0:T(4,128)} copy(f32[3,24576]{1,0:T(4,128)S(1)} %copy-done) | data formatting | bytes 589824
Async XLA Ops:
  33.6 31.9 %copy-start = (f32[3,24576]{1,0:T(4,128)S(1)}, f32[3,24576]{1,0:T(4,128)}, u32[]{:S(2)}) copy-start(f32[3,24576]{1,0:T(4,128)} %get-tuple-element.24) | copy-start | bytes 884740
where the time goes:
time: 66.4 us; the launch traced here: 66.3 us
  Pallas kernels  64.9 us (98%)
  local copies, waits for them, and re-layouts  0.75 us (1%)
    pallas_call x1, Pallas kernels, body(): make_first(cells, n_row, n_col, n)(positions, moments, let_rows)  33 us
    pallas_call x1, Pallas kernels, body(): make_near(cells, n_row * n_col, n_col, n)  31.9 us

commit v1 on v0

--- a/solution.py
+++ b/solution.py
@@ -13,7 +13,6 @@
 F32 = jnp.float32
 BF16 = jnp.bfloat16
 MESH = pl.DeviceIdType.MESH
-HIGHEST = lax.Precision.HIGHEST
 VMEM_LIMIT = 58 * 1024 * 1024
 SIX = ((0, 0), (0, 1), (0, 2), (1, 1), (1, 2), (2, 2))
 NEAR_K = 48
@@ -22,6 +21,8 @@
 NEAR_S = 56
 FAR_S = 72
 COEF_S = 56
+FORMS = 6
+GROUP = 4
 TOP_UNROLL = 24
 NEAR_UNROLL = 16
 
@@ -150,65 +151,75 @@
     lax.fori_loop(0, cells, step, 0, unroll=8)
 
 
-def leaf_sections(cells, place, moment, let_rows_ref, let_ref):
-    ones = jnp.ones((CELL, CELL), F32)
-    eight = jnp.ones((8, CELL), F32)
-    padding = jnp.zeros((256 - cells, CELL), F32)
-
-    def lane_sums(plane):
-        return lax.dot_general(
-            eight,
-            jnp.concatenate([plane, padding], axis=0),
-            (((1,), (1,)), ((), ())),
-            precision=HIGHEST,
-            preferred_element_type=F32,
-        )
-
-    spread = [
-        entry - jnp.dot(entry, ones, precision=HIGHEST, preferred_element_type=F32) * (1.0 / CELL)
-        for entry in place
-    ]
-    leaf = [lane_sums(entry) * (1.0 / CELL) for entry in place]
-    leaf += [lane_sums(entry) for entry in moment]
-    leaf += [lane_sums(spread[j] * moment[i]) for j in range(3) for i in range(3)]
+def lane_iota(shape):
+    return lax.broadcasted_iota(jnp.int32, shape, len(shape) - 1)
+
+
+def spread_sums(planes, targets):
+    total = None
+    for plane, target in zip(planes, targets):
+        parts = jnp.concatenate([part.astype(BF16) for part in split3(plane)], axis=1)
+        marked = target(lane_iota((3 * CELL, CELL))).astype(F32).astype(BF16)
+        value = jnp.dot(parts, marked, preferred_element_type=F32)
+        total = value if total is None else total + value
+    return total
+
+
+def leaf_tables(place, moment):
+    mean = 1.0 / CELL
+    centres = [spread_sums([entry], [lambda l: l >= 0]) * mean for entry in place]
+    spread = [entry - centre for entry, centre in zip(place, centres)]
+    lane = lane_iota(centres[0].shape)
+    table = spread_sums(
+        moment + [spread[j] * moment[i] for j in range(3) for i in range(3)],
+        [lambda l, k=k: l == 3 + k for k in range(12)],
+    )
+    inner = (lane >= 6) & (lane < 15)
+    by_centre = jnp.zeros_like(table)
+    for j in range(3):
+        table = jnp.where(lane == j, centres[j], table)
+        by_centre = jnp.where(inner & (lane // 3 == 2 + j), centres[j], by_centre)
+    by_moment = spread_sums(
+        moment,
+        [lambda l, i=i: (l >= 6) & (l < 15) & (lax.rem(l, 3) == i) for i in range(3)],
+    )
+    return table, by_centre, by_moment
+
+
+def leaf_sections(table, let_rows_ref, let_ref):
+    cells = table.shape[0]
+    rows = jnp.concatenate([table, jnp.zeros((256 - cells, CELL), F32)], axis=0).T
     chosen = let_rows_ref[0]
     low = jnp.bitwise_and(chosen, CELL - 1)
     upper = chosen >= CELL
     for entry in range(15):
+        row = jnp.broadcast_to(rows[entry : entry + 1, :], (8, 256))
         let_ref[:, entry, :] = jnp.where(
             upper,
-            jnp.take_along_axis(leaf[entry][:, CELL:], low, axis=1),
-            jnp.take_along_axis(leaf[entry][:, :CELL], low, axis=1),
+            jnp.take_along_axis(row[:, CELL:], low, axis=1),
+            jnp.take_along_axis(row[:, :CELL], low, axis=1),
         )
     let_ref[:, 15, :] = jnp.zeros((8, CELL), F32)
 
 
-def top_tables(cells, place, moment, top_ref, centre_ref):
-    half = cells // 2
+def top_tables(table, by_centre, by_moment, top_ref, centre_ref):
+    half = table.shape[0] // 2
     sublane = lax.broadcasted_iota(jnp.int32, (8, CELL), 0)
-    lane = lax.broadcasted_iota(jnp.int32, (8, CELL), 1)
+    lane = lane_iota((1, CELL))
     tile = jnp.zeros((8, CELL), F32)
-    centres = []
-
-    def total(plane):
-        column = jnp.sum(plane, axis=0, keepdims=True)
-        return jnp.sum(column, axis=1, keepdims=True)
-
+    middle = jnp.zeros((1, CELL), F32)
     for top in range(2):
         part = slice(top * half, (top + 1) * half)
-        centre = [total(place[i][part]) * (1.0 / (half * CELL)) for i in range(3)]
-        entries = list(centre) + [total(moment[i][part]) for i in range(3)]
-        for j in range(3):
-            offset = place[j][part] - centre[j]
-            entries += [total(offset * moment[i][part]) for i in range(3)]
-        for entry in range(15):
-            tile = jnp.where((sublane == top) & (lane == entry), entries[entry], tile)
-        centres.append(centre)
+        total = jnp.sum(table[part], axis=0, keepdims=True)
+        centre = jnp.sum(by_centre[part], axis=0, keepdims=True) * (1.0 / half)
+        moved = jnp.sum((by_centre[part] - centre) * by_moment[part], axis=0, keepdims=True)
+        row = jnp.where(lane < 3, total * (1.0 / half), total + moved)
+        tile = jnp.where(sublane == top, row, tile)
+        middle = middle + 0.5 * row
     top_ref[...] = tile
-    middle = jnp.zeros((8, CELL), F32)
     for i in range(3):
-        middle = jnp.where(sublane == i, 0.5 * (centres[0][i] + centres[1][i]), middle)
-    centre_ref[...] = middle
+        centre_ref[i : i + 1, :] = jnp.broadcast_to(middle[:, i : i + 1], (1, CELL))
+    centre_ref[3:8, :] = jnp.zeros((5, CELL), F32)
 
 
 def first_kernel(
@@ -229,10 +240,10 @@
     top_in,
     feats,
     forms_rows,
+    forms_stage,
     forms,
     coeffs,
     sums,
-    field,
     side_send,
     side_recv,
     let_send,
@@ -252,30 +263,25 @@
     def flip(value, bit):
         return value + (1 << bit) * (1 - 2 * lax.rem(value // (1 << bit), 2))
 
+    def flip_by(value, mask):
+        for bit in range(mask.bit_length()):
+            if mask >> bit & 1:
+                value = flip(value, bit)
+        return value
+
     def place_of(index):
         return (index // n_col, lax.rem(index, n_col))
 
     following = place_of(lax.rem(device + 1, devices))
     preceding = place_of(lax.rem(device + devices - 1, devices))
 
+    four = [flip_by(col, k) for k in range(1, GROUP)]
+    groups = [flip_by(col, k * GROUP) for k in range(1, n_col // GROUP)]
     barrier = pltpu.get_barrier_semaphore()
-
-    def greet(step, carry):
-        other = lax.rem(col + step, n_col)
-        pl.semaphore_signal(barrier, inc=1, device_id=(row, other), device_id_type=MESH)
-        return carry
-
-    lax.fori_loop(1, n_col, greet, 0)
-    for bit in range(row_bits):
-        pl.semaphore_signal(barrier, inc=1, device_id=(flip(row, bit), col), device_id_type=MESH)
-
-    @pl.when(col == 0)
-    def _():
-        pl.semaphore_signal(barrier, inc=1, device_id=preceding, device_id_type=MESH)
-
-    @pl.when(col == n_col - 1)
-    def _():
-        pl.semaphore_signal(barrier, inc=1, device_id=following, device_id_type=MESH)
+    partners = [(row, other) for other in four + groups]
+    partners += [(flip(row, bit), col) for bit in range(row_bits)] + [following, preceding]
+    for partner in partners:
+        pl.semaphore_signal(barrier, inc=1, device_id=partner, device_id_type=MESH)
 
     def to_planes(b, carry):
         planes_ref[pl.ds(b, 3, stride=pitch), :] = pos_ref[:, lanes(b)]
@@ -283,10 +289,6 @@
         return carry
 
     lax.fori_loop(0, cells, to_planes, 0, unroll=8)
-    top_in[col] = jnp.zeros(top_ref.shape, F32)
-
-    edge = jnp.where(col == 0, 1, 0) + jnp.where(col == n_col - 1, 1, 0)
-    pl.semaphore_wait(barrier, n_col - 1 + row_bits + edge)
 
     def side_copy(side, target, to):
         return pltpu.make_async_remote_copy(
@@ -298,35 +300,31 @@
             device_id_type=MESH,
         )
 
+    place = [planes_ref[i * pitch : i * pitch + cells, :] for i in range(3)]
+    moment = [planes_ref[(3 + i) * pitch : (3 + i) * pitch + cells, :] for i in range(3)]
+    leaf, by_centre, by_moment = leaf_tables(place, moment)
+    top_tables(leaf, by_centre, by_moment, top_ref, centre_ref)
+    top_in[col] = top_ref[...]
+    pl.semaphore_wait(barrier, len(partners))
+
+    first_copies = [
+        pltpu.make_async_remote_copy(
+            src_ref=top_ref,
+            dst_ref=top_in.at[col],
+            send_sem=top_send.at[k],
+            recv_sem=top_recv.at[k],
+            device_id=(row, other),
+            device_id_type=MESH,
+        )
+        for k, other in enumerate(four)
+    ]
+    for copy in first_copies:
+        copy.start()
     sides = [side_copy(0, before_ref, following), side_copy(1, after_ref, preceding)]
     for copy in sides:
         copy.start()
 
-    place = [planes_ref[i * pitch : i * pitch + cells, :] for i in range(3)]
-    moment = [planes_ref[(3 + i) * pitch : (3 + i) * pitch + cells, :] for i in range(3)]
-    top_tables(cells, place, moment, top_ref, centre_ref)
-
-    def top_copy(step):
-        return pltpu.make_async_remote_copy(
-            src_ref=top_ref,
-            dst_ref=top_in.at[col],
-            send_sem=top_send.at[step],
-            recv_sem=top_recv.at[step],
-            device_id=(row, lax.rem(col + step, n_col)),
-            device_id_type=MESH,
-        )
-
-    def start(step, carry):
-        top_copy(step).start()
-        return carry
-
-    def finish(step, carry):
-        top_copy(step).wait()
-        return carry
-
-    lax.fori_loop(1, n_col, start, 0)
-
-    leaf_sections(cells, place, moment, let_rows_ref, let_ref)
+    leaf_sections(leaf, let_rows_ref, let_ref)
     sections = []
     for section in range(col_bits + row_bits):
         if section < col_bits:
@@ -346,13 +344,32 @@
     for copy in sections:
         copy.start()
 
+    for copy in first_copies:
+        copy.wait()
+    mine = pl.ds(col // GROUP * GROUP, GROUP)
+    second_copies = [
+        pltpu.make_async_remote_copy(
+            src_ref=top_in.at[mine],
+            dst_ref=top_in.at[mine],
+            send_sem=top_send.at[len(four) + k],
+            recv_sem=top_recv.at[len(four) + k],
+            device_id=(row, other),
+            device_id_type=MESH,
+        )
+        for k, other in enumerate(groups)
+    ]
+    for copy in second_copies:
+        copy.start()
+
     def build(group, carry):
         x = own_offsets(planes_ref, centre_ref, cells, group * 8)
         store_rows(feats, target_rows(x), group * 8, FAR_S)
         return carry
 
-    lax.fori_loop(0, cells // 8, build, 0)
-    lax.fori_loop(1, n_col, finish, 0)
+    lax.fori_loop(0, cells // 8, build, 0, unroll=2)
+    for copy in second_copies:
+        copy.wait()
+    top_in[col] = jnp.zeros(top_ref.shape, F32)
 
     table = jnp.concatenate(
         [top_in[:, top, :] for top in range(2)] + [jnp.zeros((CELL - sources, CELL), F32)], axis=0
@@ -362,23 +379,25 @@
     entries = [entries[i] - centre_ref[i : i + 1, :] for i in range(3)] + entries[3:]
     square, first, second, outputs = expansion_coefficients(entries)
     zero = jnp.zeros_like(entries[0])
-    for position, form in enumerate((square, first, second)):
+    g = [[outputs[7 + SIX.index((min(i, j), max(i, j)))] for j in range(3)] for i in range(3)]
+    bent = [(-outputs[13 + i], g[i], None) for i in range(3)]
+    for position, form in enumerate([square, first, second] + bent):
+        base = position * FAR_K
         for k, value in enumerate(source_rows(form, zero)):
-            forms_rows[position * FAR_K + k : position * FAR_K + k + 1, :] = value
-    for position in range(3):
-        forms[position * sources : (position + 1) * sources, :] = (
-            forms_rows[position * FAR_K : (position + 1) * FAR_K, :].T[:sources, :].astype(BF16)
+            forms_rows[base + k : base + k + 1, :] = value
+    for position in range(FORMS):
+        value = forms_rows[position * FAR_K : (position + 1) * FAR_K, :].T
+        for tile in range(sources // 8):
+            start = (tile * FORMS + position) * 8
+            forms_stage[start : start + 8, :] = value[tile * 8 : (tile + 1) * 8, :]
+    forms[...] = forms_stage[...].astype(BF16)
+    for k, value in enumerate(entries[:3] + outputs[4:7]):
+        forms_rows[k : k + 1, :] = value
+    columns = forms_rows[0:CELL, :].T
+    for k in range(6):
+        coeffs[k * sources : (k + 1) * sources, :] = jnp.broadcast_to(
+            columns[:sources, k : k + 1], (sources, CELL)
         )
-    for k, value in enumerate(outputs):
-        for part, piece in enumerate(split3(value)):
-            forms_rows[part * OUT_K + k : part * OUT_K + k + 1, :] = piece
-    stacked = forms_rows[0 : 3 * OUT_K, 0:sources]
-    kind = lax.rem(lax.broadcasted_iota(jnp.int32, stacked.shape, 0), OUT_K)
-    pieces = []
-    for low, high in ((0, 4), (4, 7), (7, OUT_K)):
-        piece = jnp.where((kind >= low) & (kind < high), stacked, 0.0)
-        pieces += [piece, piece]
-    coeffs[...] = jnp.concatenate(pieces, axis=1).astype(BF16)
 
     def step(pair, carry):
         for sub in range(TOP_UNROLL):
@@ -391,27 +410,46 @@
                 axis=1,
             ).astype(BF16)
             values = jnp.dot(forms[...], features, preferred_element_type=F32)
-            parts = weights_of(
-                values[:sources], values[sources : 2 * sources], values[2 * sources :]
-            )
-            weights = jnp.concatenate([half for part in parts for half in split2(part)], axis=0)
-            result = jnp.dot(coeffs[...], weights, preferred_element_type=F32)
-            result = result[:OUT_K] + result[OUT_K : 2 * OUT_K] + result[2 * OUT_K :]
             for k in range(2):
-                sums[pl.ds(cell + k, OUT_K, stride=pitch), :] = result[:, k * CELL : (k + 1) * CELL]
+                totals = None
+                for tile in range(sources // 8):
+                    form = [
+                        values[
+                            (tile * FORMS + f) * 8 : (tile * FORMS + f + 1) * 8,
+                            k * CELL : (k + 1) * CELL,
+                        ]
+                        for f in range(FORMS)
+                    ]
+                    const = [
+                        coeffs[f * sources + tile * 8 : f * sources + (tile + 1) * 8, :]
+                        for f in range(6)
+                    ]
+                    weight, three, five = weights_of(*form[:3])
+                    terms = [weight] + [
+                        const[i] * weight + const[3 + i] * three + form[3 + i] * five
+                        for i in range(3)
+                    ]
+                    totals = terms if totals is None else [t + u for t, u in zip(totals, terms)]
+                for place_, value in enumerate(totals):
+                    sums[rows8((place_ * cells + cell + k) * 8), :] = value
         return carry
 
     lax.fori_loop(0, cells // (2 * TOP_UNROLL), step, 0)
 
     def finish_top(group, carry):
         x = own_offsets(planes_ref, centre_ref, cells, group * 8)
-        totals = [sums[rows8(k * pitch + group * 8), :] for k in range(OUT_K)]
-        for i, value in enumerate(expansion_fields(x, totals)):
-            field[rows8(i * pitch + group * 8), :] = value
-        return carry
-
-    lax.fori_loop(0, cells // 8, finish_top, 0)
-    planes_to_output(field, out_ref, cells)
+        totals = []
+        for place_ in range(4):
+            base = (place_ * cells + group * 8) * 8
+            parts = [sums[pl.ds(base + k, 8, stride=8), :] for k in range(8)]
+            while len(parts) > 1:
+                parts = [parts[k] + parts[k + 1] for k in range(0, len(parts), 2)]
+            totals.append(parts[0])
+        for i in range(3):
+            out_ref[rows8(i * pitch + group * 8), :] = x[i] * totals[0] - totals[1 + i]
+        return carry
+
+    lax.fori_loop(0, cells // 8, finish_top, 0, unroll=2)
 
     for copy in sections:
         copy.wait()
@@ -461,8 +499,10 @@
     centre_ref,
     far_ref,
     let_ref,
+    top_ref,
     near_out,
     let_out,
+    top_out,
     near_sources,
     near_targets,
     far_sources,
@@ -490,7 +530,7 @@
             store_rows(near_sources, near_source_rows(y, moment), first + group * 8, NEAR_S)
             return carry
 
-        lax.fori_loop(0, cells // 8, build, 0)
+        lax.fori_loop(0, cells // 8, build, 0, unroll=2)
 
     device = lax.axis_index("row") * n_col + lax.axis_index("col")
     ordinal = jnp.full((8, CELL), device, jnp.int32)
@@ -504,7 +544,7 @@
         store_rows(far_targets, target_rows(x), group * 8, FAR_S)
         return carry
 
-    lax.fori_loop(0, cells // 8, build_targets, 0)
+    lax.fori_loop(0, cells // 8, build_targets, 0, unroll=2)
 
     groups = cells // 8
     lists = far_ref[...].astype(F32)
@@ -559,7 +599,7 @@
         store_rows(far_coeffs, rows, group * 8, COEF_S)
         return carry
 
-    lax.fori_loop(0, groups, build_far, 0)
+    lax.fori_loop(0, groups, build_far, 0, unroll=2)
 
     upper_rows = lax.rem(lax.broadcasted_iota(jnp.int32, (NEAR_K, CELL), 0), 8) < 4
 
@@ -626,7 +666,7 @@
             )
         return carry
 
-    lax.fori_loop(0, cells // 8, finish_near, 0)
+    lax.fori_loop(0, cells // 8, finish_near, 0, unroll=2)
     planes_to_output(field, near_out, cells)
 
     def finish_far(group, carry):
@@ -636,15 +676,16 @@
             field[rows8(i * pitch_of(cells) + group * 8), :] = value
         return carry
 
-    lax.fori_loop(0, cells // 8, finish_far, 0)
+    lax.fori_loop(0, cells // 8, finish_far, 0, unroll=2)
     planes_to_output(field, let_out, cells)
+    planes_to_output(top_ref, top_out, cells)
 
 
 def vmem(count):
     return [pl.BlockSpec(memory_space=pltpu.VMEM)] * count
 
 
-def make_first(cells, n_row, n_col, n):
+def make_first(cells, n_row, n_col):
     bits = n_row.bit_length() + n_col.bit_length() - 2
     sources = 2 * n_col
     planes = jax.ShapeDtypeStruct((6 * pitch_of(cells), CELL), F32)
@@ -656,7 +697,7 @@
             planes,
             jax.ShapeDtypeStruct((bits, 16, CELL), F32),
             jax.ShapeDtypeStruct((8, CELL), F32),
-            jax.ShapeDtypeStruct((3, n), F32),
+            jax.ShapeDtypeStruct((3 * pitch_of(cells), CELL), F32),
         ),
         in_specs=vmem(3),
         out_specs=tuple(
@@ -667,11 +708,11 @@
             pltpu.VMEM((8, CELL), F32),
             pltpu.VMEM((n_col, 8, CELL), F32),
             pltpu.VMEM((cells * FAR_S, CELL), F32),
-            pltpu.VMEM((3 * FAR_K, CELL), F32),
-            pltpu.VMEM((3 * sources, FAR_K), BF16),
-            pltpu.VMEM((3 * OUT_K, 6 * sources), BF16),
-            pltpu.VMEM((OUT_K * pitch_of(cells), CELL), F32),
-            pltpu.VMEM((3 * pitch_of(cells), CELL), F32),
+            pltpu.VMEM((FORMS * FAR_K, CELL), F32),
+            pltpu.VMEM((FORMS * sources, FAR_K), F32),
+            pltpu.VMEM((FORMS * sources, FAR_K), BF16),
+            pltpu.VMEM((6 * sources, CELL), F32),
+            pltpu.VMEM((4 * cells * 8, CELL), F32),
             pltpu.SemaphoreType.DMA((2,)),
             pltpu.SemaphoreType.DMA((2,)),
             pltpu.SemaphoreType.DMA((bits,)),
@@ -692,9 +733,9 @@
 def make_near(cells, devices, n_col, n):
     return pl.pallas_call(
         functools.partial(near_kernel, cells, devices, n_col),
-        out_shape=(jax.ShapeDtypeStruct((3, n), F32), jax.ShapeDtypeStruct((3, n), F32)),
-        in_specs=[pl.BlockSpec(memory_space=pltpu.SMEM)] + vmem(6),
-        out_specs=tuple(vmem(2)),
+        out_shape=(jax.ShapeDtypeStruct((3, n), F32),) * 3,
+        in_specs=[pl.BlockSpec(memory_space=pltpu.SMEM)] + vmem(7),
+        out_specs=tuple(vmem(3)),
         scratch_shapes=[
             pltpu.VMEM((3 * cells * NEAR_S, CELL), F32),
             pltpu.VMEM((cells * NEAR_S, CELL), F32),
@@ -719,10 +760,10 @@
     cells = n // CELL
     n_row, n_col = lax.axis_size("row"), lax.axis_size("col")
     bits = let_rows.shape[1]
-    planes, before, after, let_in, centre, top = make_first(cells, n_row, n_col, n)(
+    planes, before, after, let_in, centre, top = make_first(cells, n_row, n_col)(
         positions, moments, let_rows
     )
-    near, remote = make_near(cells, n_row * n_col, n_col, n)(
+    return make_near(cells, n_row * n_col, n_col, n)(
         near_list.T,
         planes,
         before,
@@ -730,8 +771,8 @@
         centre,
         far_list.T,
         let_in.reshape(bits * 16, CELL),
-    )
-    return near, remote, top
+        top,
+    )
 
 
 def solution(mesh):

time: 66.4 us -> 65.2 us (0.982)
  local copies, waits for them, and re-layouts: 0.75 us -> 0 us
    unnamed x3 -> x0, local copies, waits for them, and re-layouts: 0.75 us -> none
    pallas_call x1, Pallas kernels: 31.9 us -> 31.2 us  [body(): make_near(cells, n_row * n_col, n_col, n)]
where the time goes in v1:
time: 65.2 us; the launch traced here: 65 us
  Pallas kernels  64.4 us (99%)
    pallas_call x1, Pallas kernels, body(): make_first(cells, n_row, n_col)(positions, moments, let_rows)  33.2 us
    pallas_call x1, Pallas kernels, body(): make_near(cells, n_row * n_col, n_col, n)  31.2 us

profile of v1, /device:TPU:1, one launch (start us, length us, event | category | flops | bytes accessed | tf_op | source)
XLA Modules:
  0.0 65.0 jit_solution(12923804266826442708)
XLA Ops:
  0.6 33.2 %tables_exchange_top.1 = (f32[1200,128]{1,0:T(8,128)}, f32[1200,128]{1,0:T(8,128)}, f32[1200,128]{1,0:T(8,128)}, f32[8,16,128]{2,1,0:T(8,128)}, f32[8,128]{1,0:T(8,128)}, /*index=5*/f32[600,128]{1,0:T(8,128)}) custom-call(f32[3,24576]{1,0:T(4,128)} %pos_ref.1, f32[3,24576]{1,0:T(4,128)} %mom_ref.1, s32[1,8,128]{2,1,0:T(8,128)} %let_rows_ref.1), custom_call_target="tpu_custom_call" | custom-call | flops 8000000000 | bytes 4000000 | tf_op jit(solution)/shard_map/tables_exchange_top/pallas_call | solution.py:763
  33.8 31.2 %near_and_let_field.1 = (f32[3,24576]{1,0:T(4,128)}, f32[3,24576]{1,0:T(4,128)}, f32[3,24576]{1,0:T(4,128)}) custom-call(s32[2,192]{1,0:T(2,128)} %bitcast.4, f32[1200,128]{1,0:T(8,128)} %get-tuple-element.9.own_ref, f32[1200,128]{1,0:T(8,128)} %get-tuple-element.10.prev_ref, f32[1200,128]{1,0:T(8,128)} %get-tuple-element.11.next_ref, ...), custom_call_target="tpu_custom_call" | custom-call | flops 30000001024 | bytes 4000000 | tf_op jit(solution)/shard_map/near_and_let_field/pallas_call | solution.py:766

commit v2 on v1

--- a/solution.py
+++ b/solution.py
@@ -24,7 +24,7 @@
 FORMS = 6
 GROUP = 4
 TOP_UNROLL = 24
-NEAR_UNROLL = 16
+NEAR_UNROLL = 32
 
 
 def split3(value):
@@ -290,12 +290,13 @@
 
     lax.fori_loop(0, cells, to_planes, 0, unroll=8)
 
-    def side_copy(side, target, to):
+    def side_copy(side, part, target, to):
+        rows = slice(part * pitch, (part + 1) * pitch)
         return pltpu.make_async_remote_copy(
-            src_ref=planes_ref,
-            dst_ref=target,
-            send_sem=side_send.at[side],
-            recv_sem=side_recv.at[side],
+            src_ref=planes_ref.at[rows],
+            dst_ref=target.at[rows],
+            send_sem=side_send.at[6 * side + part],
+            recv_sem=side_recv.at[6 * side + part],
             device_id=to,
             device_id_type=MESH,
         )
@@ -320,7 +321,10 @@
     ]
     for copy in first_copies:
         copy.start()
-    sides = [side_copy(0, before_ref, following), side_copy(1, after_ref, preceding)]
+    sides = []
+    for part in range(6):
+        sides.append(side_copy(0, part, before_ref, following))
+        sides.append(side_copy(1, part, after_ref, preceding))
     for copy in sides:
         copy.start()
 
@@ -713,8 +717,8 @@
             pltpu.VMEM((FORMS * sources, FAR_K), BF16),
             pltpu.VMEM((6 * sources, CELL), F32),
             pltpu.VMEM((4 * cells * 8, CELL), F32),
-            pltpu.SemaphoreType.DMA((2,)),
-            pltpu.SemaphoreType.DMA((2,)),
+            pltpu.SemaphoreType.DMA((12,)),
+            pltpu.SemaphoreType.DMA((12,)),
             pltpu.SemaphoreType.DMA((bits,)),
             pltpu.SemaphoreType.DMA((bits,)),
             pltpu.SemaphoreType.DMA((n_col,)),

time: 65.2 us -> 63.4 us (0.972)
  Pallas kernels: 64.4 us -> 62.6 us
    pallas_call x1, Pallas kernels: 31.2 us -> 29.2 us  [body(): make_near(cells, n_row * n_col, n_col, n)]
where the time goes in v2:
time: 63.4 us; the launch traced here: 63.3 us
  Pallas kernels  62.6 us (99%)
  between operations  0.64 us (1%)
    pallas_call x1, Pallas kernels, body(): make_first(cells, n_row, n_col)(positions, moments, let_rows)  33.4 us
    pallas_call x1, Pallas kernels, body(): make_near(cells, n_row * n_col, n_col, n)  29.2 us

profile of v2, /device:TPU:1, one launch (start us, length us, event | category | flops | bytes accessed | tf_op | source)
XLA Modules:
  0.0 63.3 jit_solution(11033843975237861970)
XLA Ops:
  0.6 33.4 %tables_exchange_top.1 = (f32[1200,128]{1,0:T(8,128)}, f32[1200,128]{1,0:T(8,128)}, f32[1200,128]{1,0:T(8,128)}, f32[8,16,128]{2,1,0:T(8,128)}, f32[8,128]{1,0:T(8,128)}, /*index=5*/f32[600,128]{1,0:T(8,128)}) custom-call(f32[3,24576]{1,0:T(4,128)} %pos_ref.1, f32[3,24576]{1,0:T(4,128)} %mom_ref.1, s32[1,8,128]{2,1,0:T(8,128)} %let_rows_ref.1), custom_call_target="tpu_custom_call" | custom-call | flops 8000000000 | bytes 4000000 | tf_op jit(solution)/shard_map/tables_exchange_top/pallas_call | solution.py:767
  34.1 29.2 %near_and_let_field.1 = (f32[3,24576]{1,0:T(4,128)}, f32[3,24576]{1,0:T(4,128)}, f32[3,24576]{1,0:T(4,128)}) custom-call(s32[2,192]{1,0:T(2,128)} %bitcast.4, f32[1200,128]{1,0:T(8,128)} %get-tuple-element.9.own_ref, f32[1200,128]{1,0:T(8,128)} %get-tuple-element.10.prev_ref, f32[1200,128]{1,0:T(8,128)} %get-tuple-element.11.next_ref, ...), custom_call_target="tpu_custom_call" | custom-call | flops 30000001024 | bytes 4000000 | tf_op jit(solution)/shard_map/near_and_let_field/pallas_call | solution.py:770

commit v3 on v2

--- a/solution.py
+++ b/solution.py
@@ -24,7 +24,7 @@
 FORMS = 6
 GROUP = 4
 TOP_UNROLL = 24
-NEAR_UNROLL = 32
+NEAR_UNROLL = 48
 
 
 def split3(value):
@@ -321,12 +321,6 @@
     ]
     for copy in first_copies:
         copy.start()
-    sides = []
-    for part in range(6):
-        sides.append(side_copy(0, part, before_ref, following))
-        sides.append(side_copy(1, part, after_ref, preceding))
-    for copy in sides:
-        copy.start()
 
     leaf_sections(leaf, let_rows_ref, let_ref)
     sections = []
@@ -373,6 +367,12 @@
     lax.fori_loop(0, cells // 8, build, 0, unroll=2)
     for copy in second_copies:
         copy.wait()
+    sides = []
+    for part in range(6):
+        sides.append(side_copy(0, part, before_ref, following))
+        sides.append(side_copy(1, part, after_ref, preceding))
+    for copy in sides:
+        copy.start()
     top_in[col] = jnp.zeros(top_ref.shape, F32)
 
     table = jnp.concatenate(

time: 63.4 us -> 59.9 us (0.945)
  Pallas kernels: 62.6 us -> 59.2 us
    pallas_call x1, Pallas kernels: 33.4 us -> 30.6 us  [body(): make_first(cells, n_row, n_col)(positions, moments, let_rows)]
    pallas_call x1, Pallas kernels: 29.2 us -> 28.5 us  [body(): make_near(cells, n_row * n_col, n_col, n)]
where the time goes in v3:
time: 59.9 us; the launch traced here: 59.8 us
  Pallas kernels  59.2 us (99%)
  between operations  0.64 us (1%)
    pallas_call x1, Pallas kernels, body(): make_first(cells, n_row, n_col)(positions, moments, let_rows)  30.6 us
    pallas_call x1, Pallas kernels, body(): make_near(cells, n_row * n_col, n_col, n)  28.5 us

profile of v3, /device:TPU:1, one launch (start us, length us, event | category | flops | bytes accessed | tf_op | source)
XLA Modules:
  0.0 59.8 jit_solution(4312750890340397817)
XLA Ops:
  0.6 30.6 %tables_exchange_top.1 = (f32[1200,128]{1,0:T(8,128)}, f32[1200,128]{1,0:T(8,128)}, f32[1200,128]{1,0:T(8,128)}, f32[8,16,128]{2,1,0:T(8,128)}, f32[8,128]{1,0:T(8,128)}, /*index=5*/f32[600,128]{1,0:T(8,128)}) custom-call(f32[3,24576]{1,0:T(4,128)} %pos_ref.1, f32[3,24576]{1,0:T(4,128)} %mom_ref.1, s32[1,8,128]{2,1,0:T(8,128)} %let_rows_ref.1), custom_call_target="tpu_custom_call" | custom-call | flops 8000000000 | bytes 4000000 | tf_op jit(solution)/shard_map/tables_exchange_top/pallas_call | solution.py:767
  31.3 28.5 %near_and_let_field.1 = (f32[3,24576]{1,0:T(4,128)}, f32[3,24576]{1,0:T(4,128)}, f32[3,24576]{1,0:T(4,128)}) custom-call(s32[2,192]{1,0:T(2,128)} %bitcast.4, f32[1200,128]{1,0:T(8,128)} %get-tuple-element.9.own_ref, f32[1200,128]{1,0:T(8,128)} %get-tuple-element.10.prev_ref, f32[1200,128]{1,0:T(8,128)} %get-tuple-element.11.next_ref, ...), custom_call_target="tpu_custom_call" | custom-call | flops 30000001024 | bytes 4000000 | tf_op jit(solution)/shard_map/near_and_let_field/pallas_call | solution.py:770

commit v4 on v3

--- a/solution.py
+++ b/solution.py
@@ -25,6 +25,7 @@
 GROUP = 4
 TOP_UNROLL = 24
 NEAR_UNROLL = 48
+FAR_UNROLL = 32
 
 
 def split3(value):
@@ -229,12 +230,14 @@
     pos_ref,
     mom_ref,
     let_rows_ref,
+    far_ref,
     planes_ref,
     before_ref,
     after_ref,
+    centre_ref,
+    let_out_ref,
+    out_ref,
     let_in,
-    centre_ref,
-    out_ref,
     let_ref,
     top_ref,
     top_in,
@@ -244,6 +247,9 @@
     forms,
     coeffs,
     sums,
+    far_sources,
+    far_coeffs,
+    far_sums,
     side_send,
     side_recv,
     let_send,
@@ -440,115 +446,10 @@
 
     lax.fori_loop(0, cells // (2 * TOP_UNROLL), step, 0)
 
-    def finish_top(group, carry):
-        x = own_offsets(planes_ref, centre_ref, cells, group * 8)
-        totals = []
-        for place_ in range(4):
-            base = (place_ * cells + group * 8) * 8
-            parts = [sums[pl.ds(base + k, 8, stride=8), :] for k in range(8)]
-            while len(parts) > 1:
-                parts = [parts[k] + parts[k + 1] for k in range(0, len(parts), 2)]
-            totals.append(parts[0])
-        for i in range(3):
-            out_ref[rows8(i * pitch + group * 8), :] = x[i] * totals[0] - totals[1 + i]
-        return carry
-
-    lax.fori_loop(0, cells // 8, finish_top, 0, unroll=2)
-
     for copy in sections:
         copy.wait()
-    for copy in sides:
-        copy.wait()
-
-
-def near_source_rows(y, moment):
-    zero = jnp.zeros_like(y[0])
-    one = jnp.ones_like(y[0])
-    back = [split3(-2.0 * entry) for entry in y]
-    square = split3(y[0] * y[0] + y[1] * y[1] + y[2] * y[2] + SOFTEN)
-    scaled = [(3.0 * COUPLING) * entry for entry in moment]
-    const = split3(-(y[0] * scaled[0] + y[1] * scaled[1] + y[2] * scaled[2]))
-    scaled = [split3(entry) for entry in scaled]
-    rows = []
-    for part in range(3):
-        rows += [one] + [b[part] for b in back] + [s[part] for s in scaled] + [const[part]]
-    for part, source in ((0, 0), (1, 1), (2, 0)):
-        rows += [square[part]] + [b[source] for b in back] + [s[source] for s in scaled] + [zero]
-    return rows
-
-
-def near_target_rows(x):
-    one = jnp.ones_like(x[0])
-    zero = jnp.zeros_like(x[0])
-    norm = split3(x[0] * x[0] + x[1] * x[1] + x[2] * x[2])
-    pieces = [split3(entry) for entry in x]
-    rows = []
-    for part in range(3):
-        high = [p[0] for p in pieces]
-        rows += [norm[part]] + high + high + [one]
-    for target in (1, 1, 2):
-        chosen = [p[target] for p in pieces]
-        rows += [one] + chosen + chosen + [zero]
-    return rows
-
-
-def near_kernel(
-    cells,
-    devices,
-    n_col,
-    near_ref,
-    own_ref,
-    prev_ref,
-    next_ref,
-    centre_ref,
-    far_ref,
-    let_ref,
-    top_ref,
-    near_out,
-    let_out,
-    top_out,
-    near_sources,
-    near_targets,
-    far_sources,
-    far_coeffs,
-    far_targets,
-    masks,
-    near_sums,
-    far_sums,
-    field,
-):
     sublane = lax.broadcasted_iota(jnp.int32, (8, CELL), 0)
     lane = lax.broadcasted_iota(jnp.int32, (8, CELL), 1)
-    diagonal = lax.broadcasted_iota(jnp.int32, (CELL, CELL), 0) == lax.broadcasted_iota(
-        jnp.int32, (CELL, CELL), 1
-    )
-    masks[0:CELL, :] = jnp.zeros((CELL, CELL), F32)
-    masks[CELL : 2 * CELL, :] = jnp.where(diagonal, 1e30, 0.0)
-
-    def build_sources(ref, first, keep):
-        def build(group, carry):
-            y = own_offsets(ref, centre_ref, cells, group * 8)
-            moment = [ref[rows8((3 + i) * pitch_of(cells) + group * 8), :] for i in range(3)]
-            if keep is not None:
-                moment = [jnp.where(keep, entry, 0.0) for entry in moment]
-            store_rows(near_sources, near_source_rows(y, moment), first + group * 8, NEAR_S)
-            return carry
-
-        lax.fori_loop(0, cells // 8, build, 0, unroll=2)
-
-    device = lax.axis_index("row") * n_col + lax.axis_index("col")
-    ordinal = jnp.full((8, CELL), device, jnp.int32)
-    build_sources(prev_ref, 0, ordinal > 0)
-    build_sources(own_ref, cells, None)
-    build_sources(next_ref, 2 * cells, ordinal < devices - 1)
-
-    def build_targets(group, carry):
-        x = own_offsets(own_ref, centre_ref, cells, group * 8)
-        store_rows(near_targets, near_target_rows(x), group * 8, NEAR_S)
-        store_rows(far_targets, target_rows(x), group * 8, FAR_S)
-        return carry
-
-    lax.fori_loop(0, cells // 8, build_targets, 0, unroll=2)
 
     groups = cells // 8
     lists = far_ref[...].astype(F32)
@@ -566,7 +467,7 @@
     section = jnp.right_shift(listed, 7)
     dense = []
     for entry in range(15):
-        table = let_ref[pl.ds(entry, 8, stride=16), :]
+        table = let_in[:, entry, :]
         value = jnp.zeros(listed.shape, F32)
         for k in range(8):
             source = jnp.broadcast_to(table[k : k + 1, :], listed.shape)
@@ -604,6 +505,133 @@
         return carry
 
     lax.fori_loop(0, groups, build_far, 0, unroll=2)
+
+    def far_part(cell):
+        source = far_sources[pl.ds(pl.multiple_of(cell * FAR_S, FAR_S), FAR_K), :]
+        features = feats[pl.ds(pl.multiple_of(cell * FAR_S, FAR_S), FAR_K), :].astype(BF16)
+        values = jnp.dot(source.astype(BF16).T[:48], features, preferred_element_type=F32)
+        parts = weights_of(values[:16], values[16:32], values[32:48])
+        weights = jnp.concatenate([half for part in parts for half in split2(part)], axis=0)
+        coeffs = far_coeffs[pl.ds(pl.multiple_of(cell * COEF_S, COEF_S), 48), :][:, :96].astype(BF16)
+        result = jnp.dot(coeffs, weights, preferred_element_type=F32)
+        result = result[:OUT_K] + result[OUT_K : 2 * OUT_K] + result[2 * OUT_K :]
+        far_sums[pl.ds(cell, OUT_K, stride=pitch_of(cells)), :] = result
+
+    def finish_top(group, carry):
+        x = own_offsets(planes_ref, centre_ref, cells, group * 8)
+        totals = []
+        for place_ in range(4):
+            base = (place_ * cells + group * 8) * 8
+            parts = [sums[pl.ds(base + k, 8, stride=8), :] for k in range(8)]
+            while len(parts) > 1:
+                parts = [parts[k] + parts[k + 1] for k in range(0, len(parts), 2)]
+            totals.append(parts[0])
+        for i in range(3):
+            out_ref[rows8(i * pitch + group * 8), :] = x[i] * totals[0] - totals[1 + i]
+        return carry
+
+    lax.fori_loop(0, cells // 8, finish_top, 0, unroll=2)
+
+    def far_step(part, carry):
+        for sub in range(FAR_UNROLL):
+            far_part(FAR_UNROLL * part + sub)
+        return carry
+
+    lax.fori_loop(0, cells // FAR_UNROLL, far_step, 0)
+
+    def finish_far(group, carry):
+        x = own_offsets(planes_ref, centre_ref, cells, group * 8)
+        totals = [far_sums[rows8(k * pitch_of(cells) + group * 8), :] for k in range(OUT_K)]
+        for i, value in enumerate(expansion_fields(x, totals)):
+            let_out_ref[rows8(i * pitch_of(cells) + group * 8), :] = value
+        return carry
+
+    lax.fori_loop(0, cells // 8, finish_far, 0, unroll=2)
+    for copy in sides:
+        copy.wait()
+
+
+def near_source_rows(y, moment):
+    zero = jnp.zeros_like(y[0])
+    one = jnp.ones_like(y[0])
+    back = [split3(-2.0 * entry) for entry in y]
+    square = split3(y[0] * y[0] + y[1] * y[1] + y[2] * y[2] + SOFTEN)
+    scaled = [(3.0 * COUPLING) * entry for entry in moment]
+    const = split3(-(y[0] * scaled[0] + y[1] * scaled[1] + y[2] * scaled[2]))
+    scaled = [split3(entry) for entry in scaled]
+    rows = []
+    for part in range(3):
+        rows += [one] + [b[part] for b in back] + [s[part] for s in scaled] + [const[part]]
+    for part, source in ((0, 0), (1, 1), (2, 0)):
+        rows += [square[part]] + [b[source] for b in back] + [s[source] for s in scaled] + [zero]
+    return rows
+
+
+def near_target_rows(x):
+    one = jnp.ones_like(x[0])
+    zero = jnp.zeros_like(x[0])
+    norm = split3(x[0] * x[0] + x[1] * x[1] + x[2] * x[2])
+    pieces = [split3(entry) for entry in x]
+    rows = []
+    for part in range(3):
+        high = [p[0] for p in pieces]
+        rows += [norm[part]] + high + high + [one]
+    for target in (1, 1, 2):
+        chosen = [p[target] for p in pieces]
+        rows += [one] + chosen + chosen + [zero]
+    return rows
+
+
+def near_kernel(
+    cells,
+    devices,
+    n_col,
+    near_ref,
+    own_ref,
+    prev_ref,
+    next_ref,
+    centre_ref,
+    let_planes_ref,
+    top_ref,
+    near_out,
+    let_out,
+    top_out,
+    near_sources,
+    near_targets,
+    masks,
+    near_sums,
+    field,
+):
+    sublane = lax.broadcasted_iota(jnp.int32, (8, CELL), 0)
+    diagonal = lax.broadcasted_iota(jnp.int32, (CELL, CELL), 0) == lax.broadcasted_iota(
+        jnp.int32, (CELL, CELL), 1
+    )
+    masks[0:CELL, :] = jnp.zeros((CELL, CELL), F32)
+    masks[CELL : 2 * CELL, :] = jnp.where(diagonal, 1e30, 0.0)
+
+    def build_sources(ref, first, keep):
+        def build(group, carry):
+            y = own_offsets(ref, centre_ref, cells, group * 8)
+            moment = [ref[rows8((3 + i) * pitch_of(cells) + group * 8), :] for i in range(3)]
+            if keep is not None:
+                moment = [jnp.where(keep, entry, 0.0) for entry in moment]
+            store_rows(near_sources, near_source_rows(y, moment), first + group * 8, NEAR_S)
+            return carry
+
+        lax.fori_loop(0, cells // 8, build, 0, unroll=2)
+
+    device = lax.axis_index("row") * n_col + lax.axis_index("col")
+    ordinal = jnp.full((8, CELL), device, jnp.int32)
+    build_sources(prev_ref, 0, ordinal > 0)
+    build_sources(own_ref, cells, None)
+    build_sources(next_ref, 2 * cells, ordinal < devices - 1)
+
+    def build_targets(group, carry):
+        x = own_offsets(own_ref, centre_ref, cells, group * 8)
+        store_rows(near_targets, near_target_rows(x), group * 8, NEAR_S)
+        return carry
+
+    lax.fori_loop(0, cells // 8, build_targets, 0, unroll=2)
 
     upper_rows = lax.rem(lax.broadcasted_iota(jnp.int32, (NEAR_K, CELL), 0), 8) < 4
 
@@ -642,21 +670,9 @@
             sublane < 4, total[:, :CELL], total[:, CELL:]
         )
 
-    def far_part(cell):
-        source = far_sources[pl.ds(pl.multiple_of(cell * FAR_S, FAR_S), FAR_K), :]
-        features = far_targets[pl.ds(pl.multiple_of(cell * FAR_S, FAR_S), FAR_K), :].astype(BF16)
-        values = jnp.dot(source.astype(BF16).T[:48], features, preferred_element_type=F32)
-        parts = weights_of(values[:16], values[16:32], values[32:48])
-        weights = jnp.concatenate([half for part in parts for half in split2(part)], axis=0)
-        coeffs = far_coeffs[pl.ds(pl.multiple_of(cell * COEF_S, COEF_S), 48), :][:, :96].astype(BF16)
-        result = jnp.dot(coeffs, weights, preferred_element_type=F32)
-        result = result[:OUT_K] + result[OUT_K : 2 * OUT_K] + result[2 * OUT_K :]
-        far_sums[pl.ds(cell, OUT_K, stride=pitch_of(cells)), :] = result
-
     def step(pair, carry):
         for sub in range(NEAR_UNROLL):
             near_part(NEAR_UNROLL * pair + sub)
-            far_part(NEAR_UNROLL * pair + sub)
         return carry
 
     lax.fori_loop(0, cells // NEAR_UNROLL, step, 0)
@@ -673,15 +689,7 @@
     lax.fori_loop(0, cells // 8, finish_near, 0, unroll=2)
     planes_to_output(field, near_out, cells)
 
-    def finish_far(group, carry):
-        x = own_offsets(own_ref, centre_ref, cells, group * 8)
-        totals = [far_sums[rows8(k * pitch_of(cells) + group * 8), :] for k in range(OUT_K)]
-        for i, value in enumerate(expansion_fields(x, totals)):
-            field[rows8(i * pitch_of(cells) + group * 8), :] = value
-        return carry
-
-    lax.fori_loop(0, cells // 8, finish_far, 0, unroll=2)
-    planes_to_output(field, let_out, cells)
+    planes_to_output(let_planes_ref, let_out, cells)
     planes_to_output(top_ref, top_out, cells)
 
 
@@ -699,15 +707,16 @@
             planes,
             planes,
             planes,
-            jax.ShapeDtypeStruct((bits, 16, CELL), F32),
             jax.ShapeDtypeStruct((8, CELL), F32),
             jax.ShapeDtypeStruct((3 * pitch_of(cells), CELL), F32),
+            jax.ShapeDtypeStruct((3 * pitch_of(cells), CELL), F32),
         ),
-        in_specs=vmem(3),
+        in_specs=vmem(4),
         out_specs=tuple(
             vmem(1) + [pl.BlockSpec(memory_space=pl.ANY)] * 2 + vmem(3)
         ),
         scratch_shapes=[
+            pltpu.VMEM((bits, 16, CELL), F32),
             pltpu.VMEM((bits, 16, CELL), F32),
             pltpu.VMEM((8, CELL), F32),
             pltpu.VMEM((n_col, 8, CELL), F32),
@@ -717,6 +726,9 @@
             pltpu.VMEM((FORMS * sources, FAR_K), BF16),
             pltpu.VMEM((6 * sources, CELL), F32),
             pltpu.VMEM((4 * cells * 8, CELL), F32),
+            pltpu.VMEM((cells * FAR_S, CELL), F32),
+            pltpu.VMEM((cells * COEF_S, CELL), F32),
+            pltpu.VMEM((OUT_K * pitch_of(cells), CELL), F32),
             pltpu.SemaphoreType.DMA((12,)),
             pltpu.SemaphoreType.DMA((12,)),
             pltpu.SemaphoreType.DMA((bits,)),
@@ -738,17 +750,13 @@
     return pl.pallas_call(
         functools.partial(near_kernel, cells, devices, n_col),
         out_shape=(jax.ShapeDtypeStruct((3, n), F32),) * 3,
-        in_specs=[pl.BlockSpec(memory_space=pltpu.SMEM)] + vmem(7),
+        in_specs=[pl.BlockSpec(memory_space=pltpu.SMEM)] + vmem(6),
         out_specs=tuple(vmem(3)),
         scratch_shapes=[
             pltpu.VMEM((3 * cells * NEAR_S, CELL), F32),
             pltpu.VMEM((cells * NEAR_S, CELL), F32),
-            pltpu.VMEM((cells * FAR_S, CELL), F32),
-            pltpu.VMEM((cells * COEF_S, CELL), F32),
-            pltpu.VMEM((cells * FAR_S, CELL), F32),
             pltpu.VMEM((2 * CELL, CELL), F32),
             pltpu.VMEM((8 * pitch_of(cells), CELL), F32),
-            pltpu.VMEM((OUT_K * pitch_of(cells), CELL), F32),
             pltpu.VMEM((3 * pitch_of(cells), CELL), F32),
         ],
         compiler_params=pltpu.CompilerParams(vmem_limit_bytes=VMEM_LIMIT),
@@ -763,9 +771,8 @@
     n = positions.shape[1]
     cells = n // CELL
     n_row, n_col = lax.axis_size("row"), lax.axis_size("col")
-    bits = let_rows.shape[1]
-    planes, before, after, let_in, centre, top = make_first(cells, n_row, n_col)(
-        positions, moments, let_rows
+    planes, before, after, centre, remote, top = make_first(cells, n_row, n_col)(
+        positions, moments, let_rows, far_list.T
     )
     return make_near(cells, n_row * n_col, n_col, n)(
         near_list.T,
@@ -773,8 +780,7 @@
         before,
         after,
         centre,
-        far_list.T,
-        let_in.reshape(bits * 16, CELL),
+        remote,
         top,
     )
 

time: 59.9 us -> 60.5 us (1.010)
    pallas_call x1, Pallas kernels: 30.6 us -> 38.6 us  [body(): make_first(cells, n_row, n_col)(positions, moments, let_rows, far_list.T)]
    pallas_call x1, Pallas kernels: 28.5 us -> 21.2 us  [body(): make_near(cells, n_row * n_col, n_col, n)]
where the time goes in v4:
time: 60.5 us; the launch traced here: 60.4 us
  Pallas kernels  59.8 us (99%)
  between operations  0.64 us (1%)
    pallas_call x1, Pallas kernels, body(): make_first(cells, n_row, n_col)(positions, moments, let_rows, far_list.T)  38.6 us
    pallas_call x1, Pallas kernels, body(): make_near(cells, n_row * n_col, n_col, n)  21.2 us

profile of v4, /device:TPU:1, one launch (start us, length us, event | category | flops | bytes accessed | tf_op | source)
XLA Modules:
  0.0 60.4 jit_solution(11947562709406697777)
XLA Ops:
  0.6 38.6 %tables_exchange_top.1 = (f32[1200,128]{1,0:T(8,128)}, f32[1200,128]{1,0:T(8,128)}, f32[1200,128]{1,0:T(8,128)}, f32[8,128]{1,0:T(8,128)}, f32[600,128]{1,0:T(8,128)}, /*index=5*/f32[600,128]{1,0:T(8,128)}) custom-call(f32[3,24576]{1,0:T(4,128)} %pos_ref.1, f32[3,24576]{1,0:T(4,128)} %mom_ref.1, s32[1,8,128]{2,1,0:T(8,128)} %let_rows_ref.1, s32[16,192]{1,0:T(8,128)} %bitcast.2), custom_call_target="tpu_custom_call" | custom-call | flops 8000000000 | bytes 4000000 | tf_op jit(solution)/shard_map/tables_exchange_top/pallas_call | solution.py:774
  39.2 21.2 %near_and_let_field.1 = (f32[3,24576]{1,0:T(4,128)}, f32[3,24576]{1,0:T(4,128)}, f32[3,24576]{1,0:T(4,128)}) custom-call(s32[2,192]{1,0:T(2,128)} %bitcast.3, f32[1200,128]{1,0:T(8,128)} %get-tuple-element.9.own_ref, f32[1200,128]{1,0:T(8,128)} %get-tuple-element.10.prev_ref, f32[1200,128]{1,0:T(8,128)} %get-tuple-element.11.next_ref, ...), custom_call_target="tpu_custom_call" | custom-call | flops 30000001024 | bytes 4000000 | tf_op jit(solution)/shard_map/near_and_let_field/pallas_call | solution.py:777

commit v5 on v4

--- a/solution.py
+++ b/solution.py
@@ -477,23 +477,35 @@
     for entry in range(15):
         far_sums[entry * groups : (entry + 1) * groups, :] = dense[entry]
 
-    def build_far(group, carry):
-        table = [
-            jnp.take_along_axis(
-                jnp.broadcast_to(far_sums[pl.ds(entry * groups + group, 1), :], (8, CELL)),
-                repeat,
-                axis=1,
-            )
-            for entry in range(15)
+    paired = jnp.bitwise_and(sublane, 3) * 32 + jnp.right_shift(lane, 6) * 16
+    paired = paired + jnp.bitwise_and(lane, 15)
+    quarter = jnp.bitwise_and(lane, 63)
+
+    def listed_table(group, spread):
+        rows = [far_sums[pl.ds(entry * groups + group, 1), :] for entry in range(15)]
+        return [
+            jnp.take_along_axis(jnp.broadcast_to(row, (8, CELL)), spread, axis=1) for row in rows
         ]
-        table = [table[i] - centre_ref[i : i + 1, :] for i in range(3)] + table[3:]
-        square, first, second, outputs = expansion_coefficients(table)
+
+    def centred(table):
+        return [table[i] - centre_ref[i : i + 1, :] for i in range(3)] + table[3:]
+
+    def build_far_sources(two, carry):
+        tables = [listed_table(2 * two + k, paired) for k in range(2)]
+        table = centred([jnp.where(sublane < 4, a, b) for a, b in zip(*tables)])
+        square, first, second, _ = expansion_coefficients(table)
         zero = jnp.zeros((8, CELL), F32)
         forms = [source_rows(form, zero) for form in (square, first, second)]
         rows = [
-            jnp.where(lane < 16, a, jnp.where(lane < 32, b, c)) for a, b, c in zip(*forms)
+            jnp.where(quarter < 16, a, jnp.where(quarter < 32, b, c)) for a, b, c in zip(*forms)
         ]
-        store_rows(far_sources, rows, group * 8, FAR_S)
+        store_rows(far_sources, rows, two * 8, FAR_S)
+        return carry
+
+    lax.fori_loop(0, groups // 2, build_far_sources, 0, unroll=2)
+
+    def build_far(group, carry):
+        _, _, _, outputs = expansion_coefficients(centred(listed_table(group, repeat)))
         pieces = [split3(value) for value in outputs]
         rows = []
         for part in range(3):
@@ -506,16 +518,22 @@
 
     lax.fori_loop(0, groups, build_far, 0, unroll=2)
 
-    def far_part(cell):
-        source = far_sources[pl.ds(pl.multiple_of(cell * FAR_S, FAR_S), FAR_K), :]
-        features = feats[pl.ds(pl.multiple_of(cell * FAR_S, FAR_S), FAR_K), :].astype(BF16)
-        values = jnp.dot(source.astype(BF16).T[:48], features, preferred_element_type=F32)
-        parts = weights_of(values[:16], values[16:32], values[32:48])
-        weights = jnp.concatenate([half for part in parts for half in split2(part)], axis=0)
-        coeffs = far_coeffs[pl.ds(pl.multiple_of(cell * COEF_S, COEF_S), 48), :][:, :96].astype(BF16)
-        result = jnp.dot(coeffs, weights, preferred_element_type=F32)
-        result = result[:OUT_K] + result[OUT_K : 2 * OUT_K] + result[2 * OUT_K :]
-        far_sums[pl.ds(cell, OUT_K, stride=pitch_of(cells)), :] = result
+    def far_pair(cell):
+        source = far_sources[pl.ds(pl.multiple_of(cell // 2 * FAR_S, FAR_S), FAR_K), :]
+        turned = source.astype(BF16).T
+        for k in range(2):
+            start = (cell + k) * FAR_S
+            features = feats[pl.ds(pl.multiple_of(start, FAR_S), FAR_K), :].astype(BF16)
+            values = jnp.dot(
+                turned[64 * k : 64 * k + 48], features, preferred_element_type=F32
+            )
+            parts = weights_of(values[:16], values[16:32], values[32:48])
+            weights = jnp.concatenate([half for part in parts for half in split2(part)], axis=0)
+            start = (cell + k) * COEF_S
+            rows = far_coeffs[pl.ds(pl.multiple_of(start, COEF_S), 48), :][:, :96].astype(BF16)
+            result = jnp.dot(rows, weights, preferred_element_type=F32)
+            result = result[:OUT_K] + result[OUT_K : 2 * OUT_K] + result[2 * OUT_K :]
+            far_sums[pl.ds(cell + k, OUT_K, stride=pitch), :] = result
 
     def finish_top(group, carry):
         x = own_offsets(planes_ref, centre_ref, cells, group * 8)
@@ -533,8 +551,8 @@
     lax.fori_loop(0, cells // 8, finish_top, 0, unroll=2)
 
     def far_step(part, carry):
-        for sub in range(FAR_UNROLL):
-            far_part(FAR_UNROLL * part + sub)
+        for sub in range(0, FAR_UNROLL, 2):
+            far_pair(FAR_UNROLL * part + sub)
         return carry
 
     lax.fori_loop(0, cells // FAR_UNROLL, far_step, 0)
@@ -726,7 +744,7 @@
             pltpu.VMEM((FORMS * sources, FAR_K), BF16),
             pltpu.VMEM((6 * sources, CELL), F32),
             pltpu.VMEM((4 * cells * 8, CELL), F32),
-            pltpu.VMEM((cells * FAR_S, CELL), F32),
+            pltpu.VMEM((cells // 2 * FAR_S, CELL), F32),
             pltpu.VMEM((cells * COEF_S, CELL), F32),
             pltpu.VMEM((OUT_K * pitch_of(cells), CELL), F32),
             pltpu.SemaphoreType.DMA((12,)),

time: 60.5 us -> 60.7 us (level)
  no operation moved by 1% of the time
where the time goes in v5:
time: 60.7 us; the launch traced here: 60.6 us
  Pallas kernels  59.9 us (99%)
  between operations  0.64 us (1%)
    pallas_call x1, Pallas kernels, body(): make_first(cells, n_row, n_col)(positions, moments, let_rows, far_list.T)  38.8 us
    pallas_call x1, Pallas kernels, body(): make_near(cells, n_row * n_col, n_col, n)  21.2 us

profile of v5, /device:TPU:1, one launch (start us, length us, event | category | flops | bytes accessed | tf_op | source)
XLA Modules:
  0.0 60.6 jit_solution(17771059668262358166)
XLA Ops:
  0.6 38.8 %tables_exchange_top.1 = (f32[1200,128]{1,0:T(8,128)}, f32[1200,128]{1,0:T(8,128)}, f32[1200,128]{1,0:T(8,128)}, f32[8,128]{1,0:T(8,128)}, f32[600,128]{1,0:T(8,128)}, /*index=5*/f32[600,128]{1,0:T(8,128)}) custom-call(f32[3,24576]{1,0:T(4,128)} %pos_ref.1, f32[3,24576]{1,0:T(4,128)} %mom_ref.1, s32[1,8,128]{2,1,0:T(8,128)} %let_rows_ref.1, s32[16,192]{1,0:T(8,128)} %bitcast.2), custom_call_target="tpu_custom_call" | custom-call | flops 8000000000 | bytes 4000000 | tf_op jit(solution)/shard_map/tables_exchange_top/pallas_call | solution.py:792
  39.4 21.2 %near_and_let_field.1 = (f32[3,24576]{1,0:T(4,128)}, f32[3,24576]{1,0:T(4,128)}, f32[3,24576]{1,0:T(4,128)}) custom-call(s32[2,192]{1,0:T(2,128)} %bitcast.3, f32[1200,128]{1,0:T(8,128)} %get-tuple-element.9.own_ref, f32[1200,128]{1,0:T(8,128)} %get-tuple-element.10.prev_ref, f32[1200,128]{1,0:T(8,128)} %get-tuple-element.11.next_ref, ...), custom_call_target="tpu_custom_call" | custom-call | flops 30000001024 | bytes 4000000 | tf_op jit(solution)/shard_map/near_and_let_field/pallas_call | solution.py:795

commit v6 on v3

--- a/solution.py
+++ b/solution.py
@@ -155,11 +155,11 @@
     return lax.broadcasted_iota(jnp.int32, shape, len(shape) - 1)
 
 
-def spread_sums(planes, targets):
+def spread_sums(planes, targets, terms):
     total = None
     for plane, target in zip(planes, targets):
-        parts = jnp.concatenate([part.astype(BF16) for part in split3(plane)], axis=1)
-        marked = target(lane_iota((3 * CELL, CELL))).astype(F32).astype(BF16)
+        parts = jnp.concatenate([part.astype(BF16) for part in split3(plane)[:terms]], axis=1)
+        marked = target(lane_iota((terms * CELL, CELL))).astype(F32).astype(BF16)
         value = jnp.dot(parts, marked, preferred_element_type=F32)
         total = value if total is None else total + value
     return total
@@ -167,12 +167,13 @@
 
 def leaf_tables(place, moment):
     mean = 1.0 / CELL
-    centres = [spread_sums([entry], [lambda l: l >= 0]) * mean for entry in place]
+    centres = [spread_sums([entry], [lambda l: l >= 0], 3) * mean for entry in place]
     spread = [entry - centre for entry, centre in zip(place, centres)]
     lane = lane_iota(centres[0].shape)
     table = spread_sums(
         moment + [spread[j] * moment[i] for j in range(3) for i in range(3)],
         [lambda l, k=k: l == 3 + k for k in range(12)],
+        2,
     )
     inner = (lane >= 6) & (lane < 15)
     by_centre = jnp.zeros_like(table)
@@ -182,6 +183,7 @@
     by_moment = spread_sums(
         moment,
         [lambda l, i=i: (l >= 6) & (l < 15) & (lax.rem(l, 3) == i) for i in range(3)],
+        2,
     )
     return table, by_centre, by_moment
 
@@ -358,20 +360,22 @@
     ]
     for copy in second_copies:
         copy.start()
-
-    def build(group, carry):
-        x = own_offsets(planes_ref, centre_ref, cells, group * 8)
-        store_rows(feats, target_rows(x), group * 8, FAR_S)
-        return carry
-
-    lax.fori_loop(0, cells // 8, build, 0, unroll=2)
-    for copy in second_copies:
-        copy.wait()
     sides = []
     for part in range(6):
         sides.append(side_copy(0, part, before_ref, following))
         sides.append(side_copy(1, part, after_ref, preceding))
-    for copy in sides:
+    for copy in sides[:6]:
+        copy.start()
+
+    def build(group, carry):
+        x = own_offsets(planes_ref, centre_ref, cells, group * 8)
+        store_rows(feats, target_rows(x), group * 8, FAR_S)
+        return carry
+
+    lax.fori_loop(0, cells // 8, build, 0, unroll=2)
+    for copy in second_copies:
+        copy.wait()
+    for copy in sides[6:]:
         copy.start()
     top_in[col] = jnp.zeros(top_ref.shape, F32)
 
@@ -516,7 +520,17 @@
     near_sums,
     far_sums,
     field,
+    prev_planes,
+    next_planes,
+    fetch_sem,
 ):
+    fetches = [
+        pltpu.make_async_copy(prev_ref, prev_planes, fetch_sem.at[0]),
+        pltpu.make_async_copy(next_ref, next_planes, fetch_sem.at[1]),
+    ]
+    for fetch in fetches:
+        fetch.start()
+
     sublane = lax.broadcasted_iota(jnp.int32, (8, CELL), 0)
     lane = lax.broadcasted_iota(jnp.int32, (8, CELL), 1)
     diagonal = lax.broadcasted_iota(jnp.int32, (CELL, CELL), 0) == lax.broadcasted_iota(
@@ -538,9 +552,7 @@
 
     device = lax.axis_index("row") * n_col + lax.axis_index("col")
     ordinal = jnp.full((8, CELL), device, jnp.int32)
-    build_sources(prev_ref, 0, ordinal > 0)
     build_sources(own_ref, cells, None)
-    build_sources(next_ref, 2 * cells, ordinal < devices - 1)
 
     def build_targets(group, carry):
         x = own_offsets(own_ref, centre_ref, cells, group * 8)
@@ -604,6 +616,11 @@
         return carry
 
     lax.fori_loop(0, groups, build_far, 0, unroll=2)
+
+    for fetch in fetches:
+        fetch.wait()
+    build_sources(prev_planes, 0, ordinal > 0)
+    build_sources(next_planes, 2 * cells, ordinal < devices - 1)
 
     upper_rows = lax.rem(lax.broadcasted_iota(jnp.int32, (NEAR_K, CELL), 0), 8) < 4
 
@@ -738,7 +755,10 @@
     return pl.pallas_call(
         functools.partial(near_kernel, cells, devices, n_col),
         out_shape=(jax.ShapeDtypeStruct((3, n), F32),) * 3,
-        in_specs=[pl.BlockSpec(memory_space=pltpu.SMEM)] + vmem(7),
+        in_specs=[pl.BlockSpec(memory_space=pltpu.SMEM)]
+        + vmem(1)
+        + [pl.BlockSpec(memory_space=pl.ANY)] * 2
+        + vmem(4),
         out_specs=tuple(vmem(3)),
         scratch_shapes=[
             pltpu.VMEM((3 * cells * NEAR_S, CELL), F32),
@@ -750,6 +770,9 @@
             pltpu.VMEM((8 * pitch_of(cells), CELL), F32),
             pltpu.VMEM((OUT_K * pitch_of(cells), CELL), F32),
             pltpu.VMEM((3 * pitch_of(cells), CELL), F32),
+            pltpu.VMEM((6 * pitch_of(cells), CELL), F32),
+            pltpu.VMEM((6 * pitch_of(cells), CELL), F32),
+            pltpu.SemaphoreType.DMA((2,)),
         ],
         compiler_params=pltpu.CompilerParams(vmem_limit_bytes=VMEM_LIMIT),
         cost_estimate=pl.CostEstimate(

time: 59.9 us -> 58.9 us (0.983)
  Pallas kernels: 59.2 us -> 58.1 us
    pallas_call x1, Pallas kernels: 30.6 us -> 29.9 us  [body(): make_first(cells, n_row, n_col)(positions, moments, let_rows)]
where the time goes in v6:
time: 58.9 us; the launch traced here: 58.8 us
  Pallas kernels  58.1 us (99%)
  between operations  0.64 us (1%)
    pallas_call x1, Pallas kernels, body(): make_first(cells, n_row, n_col)(positions, moments, let_rows)  29.9 us
    pallas_call x1, Pallas kernels, body(): make_near(cells, n_row * n_col, n_col, n)  28.2 us

profile of v6, /device:TPU:1, one launch (start us, length us, event | category | flops | bytes accessed | tf_op | source)
XLA Modules:
  0.0 58.8 jit_solution(12225037513304890204)
XLA Ops:
  0.6 29.9 %tables_exchange_top.1 = (f32[1200,128]{1,0:T(8,128)}, f32[1200,128]{1,0:T(8,128)}, f32[1200,128]{1,0:T(8,128)}, f32[8,16,128]{2,1,0:T(8,128)}, f32[8,128]{1,0:T(8,128)}, /*index=5*/f32[600,128]{1,0:T(8,128)}) custom-call(f32[3,24576]{1,0:T(4,128)} %pos_ref.1, f32[3,24576]{1,0:T(4,128)} %mom_ref.1, s32[1,8,128]{2,1,0:T(8,128)} %let_rows_ref.1), custom_call_target="tpu_custom_call" | custom-call | flops 8000000000 | bytes 4000000 | tf_op jit(solution)/shard_map/tables_exchange_top/pallas_call | solution.py:790
  30.6 28.2 %near_and_let_field.1 = (f32[3,24576]{1,0:T(4,128)}, f32[3,24576]{1,0:T(4,128)}, f32[3,24576]{1,0:T(4,128)}) custom-call(s32[2,192]{1,0:T(2,128)} %bitcast.4, f32[1200,128]{1,0:T(8,128)} %get-tuple-element.9.own_ref, f32[1200,128]{1,0:T(8,128)} %get-tuple-element.10.prev_ref, f32[1200,128]{1,0:T(8,128)} %get-tuple-element.11.next_ref, ...), custom_call_target="tpu_custom_call" | custom-call | flops 30000001024 | bytes 4000000 | tf_op jit(solution)/shard_map/near_and_let_field/pallas_call | solution.py:793

commit v7 on v6

--- a/solution.py
+++ b/solution.py
@@ -22,9 +22,11 @@
 FAR_S = 72
 COEF_S = 56
 FORMS = 6
+SOURCE_KEPT = (*range(24), 24, 32, 40)
+TARGET_KEPT = (*range(8), 8, 16, *range(24, 32), *range(40, 48))
 GROUP = 4
-TOP_UNROLL = 24
-NEAR_UNROLL = 48
+TOP_UNROLL = 32
+NEAR_UNROLL = 64
 
 
 def split3(value):
@@ -132,9 +134,10 @@
     return pl.ds(pl.multiple_of(block * CELL, CELL), CELL)
 
 
-def store_rows(ref, rows, first, stride):
+def store_rows(ref, rows, first, stride, kept=None):
     for place, value in enumerate(rows):
-        ref[pl.ds(first * stride + place, 8, stride=stride), :] = value
+        if kept is None or place in kept:
+            ref[pl.ds(first * stride + place, 8, stride=stride), :] = value
 
 
 def own_offsets(planes_ref, centre_ref, cells, start):
@@ -364,7 +367,7 @@
     for part in range(6):
         sides.append(side_copy(0, part, before_ref, following))
         sides.append(side_copy(1, part, after_ref, preceding))
-    for copy in sides[:6]:
+    for copy in sides:
         copy.start()
 
     def build(group, carry):
@@ -375,8 +378,6 @@
     lax.fori_loop(0, cells // 8, build, 0, unroll=2)
     for copy in second_copies:
         copy.wait()
-    for copy in sides[6:]:
-        copy.start()
     top_in[col] = jnp.zeros(top_ref.shape, F32)
 
     table = jnp.concatenate(
@@ -545,7 +546,8 @@
             moment = [ref[rows8((3 + i) * pitch_of(cells) + group * 8), :] for i in range(3)]
             if keep is not None:
                 moment = [jnp.where(keep, entry, 0.0) for entry in moment]
-            store_rows(near_sources, near_source_rows(y, moment), first + group * 8, NEAR_S)
+            rows = near_source_rows(y, moment)
+            store_rows(near_sources, rows, first + group * 8, NEAR_S, SOURCE_KEPT)
             return carry
 
         lax.fori_loop(0, cells // 8, build, 0, unroll=2)
@@ -556,7 +558,7 @@
 
     def build_targets(group, carry):
         x = own_offsets(own_ref, centre_ref, cells, group * 8)
-        store_rows(near_targets, near_target_rows(x), group * 8, NEAR_S)
+        store_rows(near_targets, near_target_rows(x), group * 8, NEAR_S, TARGET_KEPT)
         store_rows(far_targets, target_rows(x), group * 8, FAR_S)
         return carry
 
@@ -625,14 +627,23 @@
     upper_rows = lax.rem(lax.broadcasted_iota(jnp.int32, (NEAR_K, CELL), 0), 8) < 4
 
     def near_part(cell):
-        targets = near_targets[pl.ds(pl.multiple_of(cell * NEAR_S, NEAR_S), NEAR_K), :]
+        kept = near_targets[pl.ds(pl.multiple_of(cell * NEAR_S, NEAR_S), NEAR_K), :]
+        tiles = [kept[8 * k : 8 * k + 8] for k in range(6)]
+        for k in (1, 2):
+            tiles[k] = jnp.where(sublane == 0, tiles[k], tiles[0])
+        tiles[4] = tiles[3]
+        targets = jnp.concatenate(tiles, axis=0)
         features = jnp.concatenate(
             [jnp.where(upper_rows, targets, 0.0), jnp.where(upper_rows, 0.0, targets)], axis=1
         ).astype(BF16)
         total = None
         for e in range(2):
             block = near_ref[e, cell]
-            source = near_sources[pl.ds(pl.multiple_of(block * NEAR_S, NEAR_S), NEAR_K), :]
+            kept = near_sources[pl.ds(pl.multiple_of(block * NEAR_S, NEAR_S), NEAR_K), :]
+            tiles = [kept[8 * k : 8 * k + 8] for k in range(6)]
+            for k, origin in ((3, 0), (4, 1), (5, 0)):
+                tiles[k] = jnp.where(sublane == 0, tiles[k], tiles[origin])
+            source = jnp.concatenate(tiles, axis=0)
             values = jnp.dot(source.astype(BF16).T, features, preferred_element_type=F32)
             own = (block == cells + cell).astype(jnp.int32)
             mask = masks[pl.ds(pl.multiple_of(own * CELL, CELL), CELL), :]

time: 58.9 us -> 57.5 us (0.976)
  Pallas kernels: 58.1 us -> 56.7 us
    pallas_call x1, Pallas kernels: 28.2 us -> 26.9 us  [body(): make_near(cells, n_row * n_col, n_col, n)]
where the time goes in v7:
time: 57.5 us; the launch traced here: 57.4 us
  Pallas kernels  56.7 us (99%)
  between operations  0.64 us (1%)
    pallas_call x1, Pallas kernels, body(): make_first(cells, n_row, n_col)(positions, moments, let_rows)  29.8 us
    pallas_call x1, Pallas kernels, body(): make_near(cells, n_row * n_col, n_col, n)  26.9 us

profile of v7, /device:TPU:1, one launch (start us, length us, event | category | flops | bytes accessed | tf_op | source)
XLA Modules:
  0.0 57.4 jit_solution(14457763134243083823)
XLA Ops:
  0.6 29.8 %tables_exchange_top.1 = (f32[1200,128]{1,0:T(8,128)}, f32[1200,128]{1,0:T(8,128)}, f32[1200,128]{1,0:T(8,128)}, f32[8,16,128]{2,1,0:T(8,128)}, f32[8,128]{1,0:T(8,128)}, /*index=5*/f32[600,128]{1,0:T(8,128)}) custom-call(f32[3,24576]{1,0:T(4,128)} %pos_ref.1, f32[3,24576]{1,0:T(4,128)} %mom_ref.1, s32[1,8,128]{2,1,0:T(8,128)} %let_rows_ref.1), custom_call_target="tpu_custom_call" | custom-call | flops 8000000000 | bytes 4000000 | tf_op jit(solution)/shard_map/tables_exchange_top/pallas_call | solution.py:801
  30.5 26.9 %near_and_let_field.1 = (f32[3,24576]{1,0:T(4,128)}, f32[3,24576]{1,0:T(4,128)}, f32[3,24576]{1,0:T(4,128)}) custom-call(s32[2,192]{1,0:T(2,128)} %bitcast.4, f32[1200,128]{1,0:T(8,128)} %get-tuple-element.9.own_ref, f32[1200,128]{1,0:T(8,128)} %get-tuple-element.10.prev_ref, f32[1200,128]{1,0:T(8,128)} %get-tuple-element.11.next_ref, ...), custom_call_target="tpu_custom_call" | custom-call | flops 30000001024 | bytes 4000000 | tf_op jit(solution)/shard_map/near_and_let_field/pallas_call | solution.py:804

commit v8 on v7

--- a/solution.py
+++ b/solution.py
@@ -25,8 +25,8 @@
 SOURCE_KEPT = (*range(24), 24, 32, 40)
 TARGET_KEPT = (*range(8), 8, 16, *range(24, 32), *range(40, 48))
 GROUP = 4
-TOP_UNROLL = 32
-NEAR_UNROLL = 64
+TOP_UNROLL = 48
+NEAR_UNROLL = 96
 
 
 def split3(value):

time: 57.5 us -> 57.5 us (level)
  no operation moved by 1% of the time
where the time goes in v8:
time: 57.5 us; the launch traced here: 57.3 us
  Pallas kernels  56.5 us (98%)
  between operations  0.8 us (1%)
    pallas_call x1, Pallas kernels, body(): make_first(cells, n_row, n_col)(positions, moments, let_rows)  29.8 us
    pallas_call x1, Pallas kernels, body(): make_near(cells, n_row * n_col, n_col, n)  26.8 us

profile of v8, /device:TPU:1, one launch (start us, length us, event | category | flops | bytes accessed | tf_op | source)
XLA Modules:
  0.0 57.3 jit_solution(14479509210096077760)
XLA Ops:
  0.6 29.8 %tables_exchange_top.1 = (f32[1200,128]{1,0:T(8,128)}, f32[1200,128]{1,0:T(8,128)}, f32[1200,128]{1,0:T(8,128)}, f32[8,16,128]{2,1,0:T(8,128)}, f32[8,128]{1,0:T(8,128)}, /*index=5*/f32[600,128]{1,0:T(8,128)}) custom-call(f32[3,24576]{1,0:T(4,128)} %pos_ref.1, f32[3,24576]{1,0:T(4,128)} %mom_ref.1, s32[1,8,128]{2,1,0:T(8,128)} %let_rows_ref.1), custom_call_target="tpu_custom_call" | custom-call | flops 8000000000 | bytes 4000000 | tf_op jit(solution)/shard_map/tables_exchange_top/pallas_call | solution.py:801
  30.4 26.8 %near_and_let_field.1 = (f32[3,24576]{1,0:T(4,128)}, f32[3,24576]{1,0:T(4,128)}, f32[3,24576]{1,0:T(4,128)}) custom-call(s32[2,192]{1,0:T(2,128)} %bitcast.4, f32[1200,128]{1,0:T(8,128)} %get-tuple-element.9.own_ref, f32[1200,128]{1,0:T(8,128)} %get-tuple-element.10.prev_ref, f32[1200,128]{1,0:T(8,128)} %get-tuple-element.11.next_ref, ...), custom_call_target="tpu_custom_call" | custom-call | flops 30000001024 | bytes 4000000 | tf_op jit(solution)/shard_map/near_and_let_field/pallas_call | solution.py:804
